TPU v7x, 128 devices: a whole 4x4x4 slice. The times are simulated.
128 devices in a mesh: dp: 16 (over y_lo, x, core), slab: 8 (over y_hi, z).
Axes of the slice: x: 4, y: 4 (y_hi: 2, y_lo: 2; y = y_hi * 2 + y_lo), z: 4, core: 2. Of those that a mesh axis runs over, the one named last changes fastest.
Arguments:
- latents: bfloat16 [16, 128, 512, 128], P('dp', 'slab'), may hold values from -6 to 6
- image_grad: bfloat16 [16, 3, 128, 512], P('dp', None, 'slab'), may hold values from -6 to 6
- heights: int32 [16], P('dp'), may hold values from 64 to 128, as said below
- widths: int32 [16], P('dp'), may hold values from 256 to 512, as said below
- buckets: int32 [16], P('dp'), may hold values from 0 to 7
- bucket_scale: float32 [8], replicated, may hold values from 0.5 to 2
- conv_first: bfloat16 [1152, 128], replicated, may hold values from -0.1875 to 0.1875
- conv_second: bfloat16 [1152, 128], replicated, may hold values from -0.1875 to 0.1875
- conv_image: bfloat16 [3, 1152], replicated, may hold values from -0.1875 to 0.1875
- norm_gain: float32 [128], replicated, may hold values from 0.5 to 1.5
- norm_bias: float32 [128], replicated, may hold values from -3 to 3
Outputs:
- grad_conv_first: float32 [1152, 128], P('dp')
- grad_conv_second: float32 [1152, 128], P('dp')
- grad_conv_image: float32 [3, 1152], replicated
- grad_norm_gain: float32 [128], replicated
- grad_norm_bias: float32 [128], replicated
- grad_latents: bfloat16 [16, 128, 512, 128], P('dp', 'slab')
Inputs may be any that keep to these rules, and one draw needn't show every extreme that they name: `heights`: some image has exactly 128 rows. `widths`: some image has exactly 512 columns.
All inputs are finite; a program needn't handle non-finite values.
Results may differ from a plain program's by a relative error of at most 0.0078.
Values may be sent and summed in bfloat16 or wider, within the bound.
A program may use at most 192 MiB of HBM per device.

v0:
```python
import math

import jax
import jax.numpy as jnp
from jax import lax
from jax.sharding import PartitionSpec as P

GROUPS = 32


norm_eps = 1e-06


def padded_2(block, sides, width):
    for axis, dim in sides:
        count = lax.axis_size(axis)
        forward = [(i, i + 1) for i in range(count - 1)]
        backward = [(target, source) for source, target in forward]
        low = lax.ppermute(
            lax.slice_in_dim(block, block.shape[dim] - width, None, axis=dim), axis, forward
        )
        high = lax.ppermute(lax.slice_in_dim(block, 0, width, axis=dim), axis, backward)
        block = jnp.concatenate([low, block, high], axis=dim)
    return block


def silu_slope(value):
    sigma = jax.nn.sigmoid(value)
    return sigma * (1.0 + value * (1.0 - sigma))


def conv_rows(extended, weight):
    chan_in = extended.shape[-1]
    out_rows = extended.shape[-3] - 2
    col_count = extended.shape[-2]
    padded = jnp.pad(extended, [(0, 0)] * (extended.ndim - 2) + [(1, 1), (0, 0)])
    total = jnp.zeros(extended.shape[:-3] + (out_rows, col_count, weight.shape[1]), jnp.float32)
    for tap_index in range(9):
        row_off, col_off = divmod(tap_index, 3)
        piece = padded[..., row_off : row_off + out_rows, col_off : col_off + col_count, :]
        block = weight[tap_index * chan_in : (tap_index + 1) * chan_in]
        total = total + jnp.dot(piece, block, preferred_element_type=jnp.float32)
    return total


def data_grad(extended, weight):
    chan_in = weight.shape[0] // 9
    out_rows = extended.shape[-3] - 2
    col_count = extended.shape[-2]
    padded = jnp.pad(extended, [(0, 0)] * (extended.ndim - 2) + [(1, 1), (0, 0)])
    total = jnp.zeros(extended.shape[:-3] + (out_rows, col_count, chan_in), jnp.float32)
    for tap_index in range(9):
        row_off, col_off = divmod(tap_index, 3)
        piece = padded[
            ..., 2 - row_off : 2 - row_off + out_rows, 2 - col_off : 2 - col_off + col_count, :
        ]
        block = weight[tap_index * chan_in : (tap_index + 1) * chan_in]
        total = total + jnp.dot(piece, block.T, preferred_element_type=jnp.float32)
    return total


def weight_grad(extended, cotangent):
    out_rows = extended.shape[-3] - 2
    col_count = extended.shape[-2]
    padded = jnp.pad(extended, [(0, 0)] * (extended.ndim - 2) + [(1, 1), (0, 0)])
    leading = tuple(range(cotangent.ndim - 1))
    pieces = []
    for tap_index in range(9):
        row_off, col_off = divmod(tap_index, 3)
        piece = padded[..., row_off : row_off + out_rows, col_off : col_off + col_count, :]
        pieces.append(
            lax.dot_general(
                piece, cotangent, ((leading, leading), ((), ())), preferred_element_type=jnp.float32
            )
        )
    return jnp.concatenate(pieces, axis=0)


def group_sum(values):
    summed = jnp.sum(values, axis=(1, 2))
    return summed.reshape(summed.shape[0], GROUPS, -1).sum(-1)


def silu_mask(value, inside):
    return (jax.nn.silu(value.astype(jnp.float32)) * inside[..., None]).astype(jnp.bfloat16)


def shards(
    latents,
    image_grad,
    heights,
    widths,
    buckets,
    bucket_scale,
    conv_first,
    conv_second,
    conv_image,
    norm_gain,
    norm_bias,
):
    image_count, row_count, col_count, channels = latents.shape
    per_group = channels // GROUPS
    slab_pos = lax.axis_index("slab")
    col_index = jnp.arange(col_count)
    row_index = slab_pos * row_count + jnp.arange(-0, row_count + 0)
    inside = (row_index >= 0)[None, :, None] & (row_index[None, :, None] < heights[:, None, None])
    inside = inside & (col_index[None, None, :] < widths[:, None, None])
    valid = inside.astype(jnp.float32)
    inside = valid[..., None]
    latent_f = latents.astype(jnp.float32)
    input_ext = padded_2(silu_mask(latents, valid), (("slab", 1),), 1)
    hidden_one = conv_rows(input_ext, conv_first).astype(jnp.bfloat16)
    middle_ext = padded_2(silu_mask(hidden_one, valid), (("slab", 1),), 1)
    hidden_two = latent_f + conv_rows(middle_ext, conv_second)
    hidden_one_f = hidden_one.astype(jnp.float32)
    masked = hidden_two * inside
    first_sum, square_sum = lax.psum((group_sum(masked), group_sum(masked * hidden_two)), "slab")
    count = (heights * widths * per_group).astype(jnp.float32)[:, None]
    group_mean = first_sum / count
    group_rstd = lax.rsqrt(square_sum / count - group_mean * group_mean + norm_eps)
    mean_wide = jnp.repeat(group_mean, per_group, axis=1)[:, None, None, :]
    rstd_wide = jnp.repeat(group_rstd, per_group, axis=1)[:, None, None, :]
    normed = (hidden_two - mean_wide) * rstd_wide
    shaped = normed * norm_gain + norm_bias
    norm_ext = padded_2(silu_mask(shaped, valid), (("slab", 1),), 1)
    pixel_scale = 1.0 / math.sqrt(
        image_count * lax.axis_size("dp") * row_count * lax.axis_size("slab") * col_count
    )
    bucket_count = bucket_scale.shape[0]
    picked = jnp.sum(
        jnp.where(
            buckets[:, None] == jnp.arange(bucket_count)[None, :], bucket_scale[None, :], 0.0
        ),
        axis=1,
    )
    grad_img = (
        image_grad.astype(jnp.float32) * picked[:, None, None, None] * valid[:, None]
    ).astype(jnp.bfloat16)
    grad_img_ext = padded_2(grad_img, (("slab", 2),), 1)
    norm_pad = jnp.pad(norm_ext, ((0, 0), (0, 0), (1, 1), (0, 0)))
    grad_pad = jnp.pad(grad_img_ext, ((0, 0), (0, 0), (0, 0), (1, 1)))
    image_terms = []
    grad_norm_act = jnp.zeros((image_count, row_count, col_count, channels), jnp.float32)
    for tap_index in range(9):
        row_off, col_off = divmod(tap_index, 3)
        piece = norm_pad[:, row_off : row_off + row_count, col_off : col_off + col_count, :]
        image_terms.append(
            lax.dot_general(
                grad_img,
                piece,
                (((0, 2, 3), (0, 1, 2)), ((), ())),
                preferred_element_type=jnp.float32,
            )
        )
        back_piece = grad_pad[
            :, :, 2 - row_off : 2 - row_off + row_count, 2 - col_off : 2 - col_off + col_count
        ]
        block = conv_image[:, tap_index * channels : (tap_index + 1) * channels]
        grad_norm_act = grad_norm_act + lax.dot_general(
            back_piece, block, (((1,), (0,)), ((), ())), preferred_element_type=jnp.float32
        )
    image_weight = jnp.concatenate(image_terms, axis=1)
    grad_shaped = grad_norm_act * inside * silu_slope(shaped)
    gain_term = jnp.sum(grad_shaped * normed, axis=(0, 1, 2))
    bias_term = jnp.sum(grad_shaped, axis=(0, 1, 2))
    grad_normed = grad_shaped * norm_gain
    first_back, second_back = lax.psum(
        (group_sum(grad_normed), group_sum(grad_normed * normed)), "slab"
    )
    first_wide = jnp.repeat(first_back / count, per_group, axis=1)[:, None, None, :]
    second_wide = jnp.repeat(second_back / count, per_group, axis=1)[:, None, None, :]
    grad_two = (rstd_wide * (grad_normed - first_wide - normed * second_wide) * inside).astype(
        jnp.bfloat16
    )
    grad_conv_second = weight_grad(middle_ext, grad_two)
    grad_two_ext = padded_2(grad_two, (("slab", 1),), 1)
    grad_middle = data_grad(grad_two_ext, conv_second)
    grad_one = (grad_middle * inside * silu_slope(hidden_one_f)).astype(jnp.bfloat16)
    grad_conv_first = weight_grad(input_ext, grad_one)
    grad_one_ext = padded_2(grad_one, (("slab", 1),), 1)
    grad_input = data_grad(grad_one_ext, conv_first)
    grad_latents = (
        grad_two.astype(jnp.float32) + grad_input * inside * silu_slope(latent_f)
    ).astype(jnp.bfloat16)
    gain_total, bias_total, image_total = lax.psum(
        (gain_term, bias_term, image_weight), ("dp", "slab")
    )
    stacked = jnp.stack([grad_conv_first, grad_conv_second])
    slab_total = lax.psum(stacked, "slab")
    summed = lax.psum_scatter(slab_total, "dp", scatter_dimension=1, tiled=True)
    summed = summed * pixel_scale
    return (
        summed[0],
        summed[1],
        image_total * pixel_scale,
        gain_total * pixel_scale,
        bias_total * pixel_scale,
        grad_latents,
    )


def solution(mesh):
    placed = (
        P("dp", "slab", None, None),
        P("dp", None, "slab", None),
        P("dp"),
        P("dp"),
        P("dp"),
        P(),
        P(),
        P(),
        P(),
        P(),
        P(),
    )
    return jax.shard_map(
        shards,
        mesh=mesh,
        in_specs=placed,
        out_specs=(P("dp", None), P("dp", None), P(), P(), P(), P("dp", "slab", None, None)),
        check_vma=False,
    )
```

profile of v0, /device:TPU:0, one launch (start us, length us, event | category | flops | bytes accessed | tf_op | source)
XLA Modules:
  0.0 463.0 jit_solution(13469573130334874982)
XLA Ops:
  8.6 3.2 fusion.15
  13.2 4.6 collective-permute-start
  21.0 4.5 collective-permute-start.4
  26.3 2.9 fusion.270
  29.3 2.9 fusion.248
  32.2 3.5 fusion.252
  35.7 2.9 fusion.253
  38.6 3.5 fusion.254
  42.1 2.9 fusion.255
  45.0 3.5 fusion.260
  48.5 2.9 fusion.257
  69.9 9.6 %add_convert_fusion = bf16[16,512,128]{2,1,0:T(8,128)(2,1)S(1)} fusion(f32[16,512,128]{2,1,0:T(8,128)} %fusion.117, f32[16,512,128]{2,1,0:T(8,128)S(1)} %fusion.102, f32[16,512,128]{2,1,0:T(8,128)} %fusion.100, f32[16,512,128]{2,1,0:T(8,128)S(1)} %fusion.91, f32[16,512,128]{2,1,0:T(8,128)} %fusion.98, f32[16,512,128]{2,1,0:T(8,128)} %fusion.96, ...), kind=kOutput, calls=%fused_computation.40 | convolution fusion | flops 277872640 | bytes 37781504 | tf_op jit(solution)/shard_map/dot_general | solution.py:42
  82.3 4.6 collective-permute-start.2
  86.9 3.7 fusion.281
  108.8 13.0 %fusion.1 = (f32[128]{0:T(128)S(1)}, f32[128]{0:T(128)S(1)}, f32[1,16,512,128]{3,2,1,0:T(8,128)}) fusion(f32[16,512]{1,0:T(8,128)S(1)} %and_convert_fusion, bf16[1152,128]{1,0:T(8,128)(2,1)S(1)} %copy-done.15, bf16[1,18,514,128]{3,2,1,0:T(8,128)(2,1)S(1)} %select_maximum_fusion.6, f32[16,512,128]{2,1,0:T(8,128)} %fusion.123, ...), kind=kOutput, calls=%fused_computation.12 | convolution fusion | flops 283115264 | bytes 42009600 | tf_op jit(solution)/shard_map/dot_general | solution.py:42
  122.2 29.7 %all-reduce.8 = (f32[1,32]{1,0:T(1,128)S(1)}, f32[1,32]{1,0:T(1,128)S(1)}) all-reduce(f32[1,32]{1,0:T(1,128)S(1)} %bitcast.642, f32[1,32]{1,0:T(1,128)S(1)} %bitcast.644), channel_id=1, replica_groups=mesh['dp'=16,'slab'=8] {'slab'}, use_global_device_ids=true, to_apply=%region_5.6 | all-reduce | flops 64 | bytes 512 | tf_op jit(solution)/shard_map/psum | solution.py:117
  152.3 15.4 %multiply_reduce_fusion.1 = (f32[128]{0:T(128)S(1)}, f32[128]{0:T(128)S(1)}, f32[128]{0:T(128)S(1)}, f32[128]{0:T(128)S(1)}, f32[1,16,512,128]{3,2,1,0:T(8,128)}) fusion(f32[1,16,512,128]{3,2,1,0:T(8,128)} %get-tuple-element.37, f32[128]{0:T(128)S(1)} %broadcast_in_dim.46, f32[128]{0:T(128)S(1)} %broadcast_in_dim.21, f32[128]{0:T(128)S(1)} %copy-done.27, ...), kind=kOutput, calls=%fused_computation.33 | convolution fusion | flops 35749376 | bytes 42050560 | tf_op jit(solution)/shard_map/dot_general | solution.py:159
  168.2 24.1 %all-reduce.7 = (f32[1,32]{1,0:T(1,128)S(1)}, f32[1,32]{1,0:T(1,128)S(1)}) all-reduce(f32[1,32]{1,0:T(1,128)S(1)} %bitcast.641, f32[1,32]{1,0:T(1,128)S(1)} %bitcast.643), channel_id=1, replica_groups=mesh['dp'=16,'slab'=8] {'slab'}, use_global_device_ids=true, to_apply=%region_12.13 | all-reduce | flops 64 | bytes 512 | tf_op jit(solution)/shard_map/psum | solution.py:167
  192.7 5.3 %multiply_convert_fusion = (bf16[1,16,512,128]{3,2,1,0:T(8,128)(2,1)S(1)}, bf16[1,16,512,128]{3,2,1,0:T(8,128)(2,1)S(1)}) fusion(f32[1,16,512,128]{3,2,1,0:T(8,128)} %get-tuple-element.37, f32[128]{0:T(128)S(1)} %copy-done.26, f32[128]{0:T(128)S(1)} %copy-done.27, f32[128]{0:T(128)S(1)} %broadcast_in_dim.46, f32[128]{0:T(128)S(1)} %broadcast_in_dim.21, ...), kind=kLoop, calls=%fused_computation.34 | loop fusion | flops 17825792 | bytes 12618752 | tf_op jit(solution)/shard_map/convert_element_type | solution.py:85
  215.4 5.8 %collective-permute-start.8 = (bf16[1,1,512,128]{3,2,1,0:T(8,128)(2,1)}, bf16[1,1,512,128]{3,2,1,0:T(8,128)(2,1)}, u32[]{:S(2)}, u32[]{:S(2)}) collective-permute-start(bf16[1,1,512,128]{3,2,1,0:T(8,128)(2,1)} %get-tuple-element.25), channel_id=1, source_target_pairs={{0,1},{1,2},{2,3},{3,4},{4,5},{5,6},{6,7},{8,9},{9,10},{10,11},{11... | collective-permute-start | bytes 393224 | tf_op jit(solution)/shard_map/ppermute | solution.py:19
  241.5 12.6 %fusion.10 = bf16[16,512,128]{2,1,0:T(8,128)(2,1)S(1)} fusion(bf16[16,512,128]{2,1,0:T(8,128)(2,1)S(1)} %copy-done.12, f32[16,512,128]{2,1,0:T(8,128)} %fusion.51, f32[16,512,128]{2,1,0:T(8,128)} %fusion.54, f32[16,512,128]{2,1,0:T(8,128)} %fusion.55, f32[16,512,128]{2,1,0:T(8,128)} %fusion.87, f32[16,512,128]{2,1,0:T(8,128)} %fusion.56, ...), kind=kOutput, calls=%fused_computation.21 | convolution fusion | flops 288358400 | bytes 39911424 | tf_op jit(solution)/shard_map/dot_general | solution.py:58
  273.8 72.0 %all-reduce.6 = (f32[3,1152]{1,0:T(4,128)S(1)}, f32[128]{0:T(128)S(1)}, f32[128]{0:T(128)S(1)}) all-reduce(f32[3,1152]{1,0:T(4,128)S(1)} %fusion.246, f32[128]{0:T(128)S(1)} %get-tuple-element.6, f32[128]{0:T(128)S(1)} %get-tuple-element.11), channel_id=1, replica_groups=mesh['dp'=16,'slab'=8] {'dp','slab'}, use_global_device_ids=true, to_apply=%region_15.16 | all-reduce | flops 3712 | bytes 29696 | tf_op jit(solution)/shard_map/psum | solution.py:185
  375.2 14.8 %fusion.20 = bf16[1,16,512,128]{3,2,1,0:T(8,128)(2,1)} fusion(bf16[1,16,512,128]{3,2,1,0:T(8,128)(2,1)} %param.11, f32[16,512,128]{2,1,0:T(8,128)} %fusion.23, f32[16,512,128]{2,1,0:T(8,128)} %fusion.26, f32[16,512,128]{2,1,0:T(8,128)} %fusion.27, f32[16,512,128]{2,1,0:T(8,128)} %fusion.299, f32[16,512,128]{2,1,0:T(8,128)} %fusion.28, ...), kind=kOutput, calls=%fused_computation.31 | convolution fusion | flops 290455552 | bytes 42008576 | tf_op jit(solution)/shard_map/dot_general | solution.py:58
  390.1 64.1 %all-reduce.11.cloned.1.call-done = f32[2,72,128]{2,1,0:T(8,128)} async-done(((f32[2,72,128]{2,1,0:T(8,128)}), f32[2,72,128]{2,1,0:T(8,128)}) %all-reduce.11.cloned.1.call-update) | async-done | bytes 73744 | tf_op jit(solution)/shard_map/psum | solution.py:189
  (183 shorter events, 133.9 us)
Async XLA Ops:
  7.2 368.1 %reduce-scatter.2.cloned.1.call-start = ((), (), s32[]{:S(2)}) async-start(), calls=%async_computation.1 | async-start | bytes 1253376 | tf_op jit(solution)/shard_map/reduce_scatter | solution.py:190
  8.6 16.9 %copy-start.13 = (bf16[1152,128]{1,0:T(8,128)(2,1)S(1)}, bf16[1152,128]{1,0:T(8,128)(2,1)}, u32[]{:S(2)}) copy-start(bf16[1152,128]{1,0:T(8,128)(2,1)} %param.17) | copy-start | bytes 884740
  11.8 55.4 %copy-start.2 = (bf16[1,16,512,128]{3,2,1,0:T(8,128)(2,1)}, bf16[1,16,512,128]{3,2,1,0:T(8,128)(2,1)S(1)}, u32[]{:S(2)}) copy-start(bf16[1,16,512,128]{3,2,1,0:T(8,128)(2,1)S(1)} %fusion.15) | copy-start | bytes 6291460
  11.9 39.5 %collective-permute-start.1 = (bf16[1,1,512,128]{3,2,1,0:T(8,128)(2,1)S(1)}, bf16[1,1,512,128]{3,2,1,0:T(8,128)(2,1)S(1)}, u32[]{:S(2)}, u32[]{:S(2)}) collective-permute-start(bf16[1,1,512,128]{3,2,1,0:T(8,128)(2,1)S(1)} %get-tuple-element.32), channel_id=1, source_target_pairs={{1,0},{2,1},{3,2},{4,3},{5,4},{6,5},{7,6},{9,8},{10,9},{11,10},{12... | collective-permute-start | bytes 393224 | tf_op jit(solution)/shard_map/ppermute | solution.py:22
  13.2 38.3 %collective-permute-start = (bf16[1,1,512,128]{3,2,1,0:T(8,128)(2,1)S(1)}, bf16[1,1,512,128]{3,2,1,0:T(8,128)(2,1)S(1)}, u32[]{:S(2)}, u32[]{:S(2)}) collective-permute-start(bf16[1,1,512,128]{3,2,1,0:T(8,128)(2,1)S(1)} %get-tuple-element.31), channel_id=1, source_target_pairs={{0,1},{1,2},{2,3},{3,4},{4,5},{5,6},{6,7},{8,9},{9,10},{10,11},{11... | collective-permute-start | bytes 393224 | tf_op jit(solution)/shard_map/ppermute | solution.py:19
  19.7 9.5 %collective-permute-start.5 = (bf16[1,3,1,512]{3,1,2,0:T(4,128)(2,1)S(1)}, bf16[1,3,1,512]{3,1,2,0:T(4,128)(2,1)S(1)}, u32[]{:S(2)}, u32[]{:S(2)}) collective-permute-start(bf16[1,3,1,512]{3,1,2,0:T(4,128)(2,1)S(1)} %get-tuple-element.36), channel_id=1, source_target_pairs={{1,0},{2,1},{3,2},{4,3},{5,4},{6,5},{7,6},{9,8},{10,9},{11,10},{12... | collective-permute-start | bytes 9224 | tf_op jit(solution)/shard_map/ppermute | solution.py:22
  21.0 8.2 %collective-permute-start.4 = (bf16[1,3,1,512]{3,1,2,0:T(4,128)(2,1)S(1)}, bf16[1,3,1,512]{3,1,2,0:T(4,128)(2,1)S(1)}, u32[]{:S(2)}, u32[]{:S(2)}) collective-permute-start(bf16[1,3,1,512]{3,1,2,0:T(4,128)(2,1)S(1)} %get-tuple-element.35), channel_id=1, source_target_pairs={{0,1},{1,2},{2,3},{3,4},{4,5},{5,6},{6,7},{8,9},{9,10},{10,11},{11... | collective-permute-start | bytes 9224 | tf_op jit(solution)/shard_map/ppermute | solution.py:19
  51.4 15.8 %copy-start.18 = (bf16[1,1,512,128]{3,2,1,0:T(8,128)(2,1)}, bf16[1,1,512,128]{3,2,1,0:T(8,128)(2,1)S(1)}, u32[]{:S(2)}) copy-start(bf16[1,1,512,128]{3,2,1,0:T(8,128)(2,1)S(1)} %collective-permute-done) | copy-start | bytes 393220
  53.1 16.8 %copy-start = (bf16[1,18,514,128]{3,2,1,0:T(8,128)(2,1)}, bf16[1,18,514,128]{3,2,1,0:T(8,128)(2,1)S(1)}, u32[]{:S(2)}) copy-start(bf16[1,18,514,128]{3,2,1,0:T(8,128)(2,1)S(1)} %select_maximum_fusion.8) | copy-start | bytes 7105540
  81.0 25.2 %copy-start.6 = (bf16[1,16,512,128]{3,2,1,0:T(8,128)(2,1)}, bf16[1,16,512,128]{3,2,1,0:T(8,128)(2,1)S(1)}, u32[]{:S(2)}) copy-start(bf16[1,16,512,128]{3,2,1,0:T(8,128)(2,1)S(1)} %fusion.383) | copy-start | bytes 6291460
  81.0 9.6 %collective-permute-start.3 = (bf16[1,1,512,128]{3,2,1,0:T(8,128)(2,1)S(1)}, bf16[1,1,512,128]{3,2,1,0:T(8,128)(2,1)S(1)}, u32[]{:S(2)}, u32[]{:S(2)}) collective-permute-start(bf16[1,1,512,128]{3,2,1,0:T(8,128)(2,1)S(1)} %get-tuple-element.30), channel_id=1, source_target_pairs={{1,0},{2,1},{3,2},{4,3},{5,4},{6,5},{7,6},{9,8},{10,9},{11,10},{12... | collective-permute-start | bytes 393224 | tf_op jit(solution)/shard_map/ppermute | solution.py:22
  82.3 8.3 %collective-permute-start.2 = (bf16[1,1,512,128]{3,2,1,0:T(8,128)(2,1)S(1)}, bf16[1,1,512,128]{3,2,1,0:T(8,128)(2,1)S(1)}, u32[]{:S(2)}, u32[]{:S(2)}) collective-permute-start(bf16[1,1,512,128]{3,2,1,0:T(8,128)(2,1)S(1)} %get-tuple-element.29), channel_id=1, source_target_pairs={{0,1},{1,2},{2,3},{3,4},{4,5},{5,6},{6,7},{8,9},{9,10},{10,11},{11... | collective-permute-start | bytes 393224 | tf_op jit(solution)/shard_map/ppermute | solution.py:19
  90.6 15.5 %copy-start.22 = (bf16[1,1,512,128]{3,2,1,0:T(8,128)(2,1)}, bf16[1,1,512,128]{3,2,1,0:T(8,128)(2,1)S(1)}, u32[]{:S(2)}) copy-start(bf16[1,1,512,128]{3,2,1,0:T(8,128)(2,1)S(1)} %collective-permute-done.2) | copy-start | bytes 393220
  108.8 43.6 %copy-start.26 = (f32[128]{0:T(128)S(1)}, f32[128]{0:T(128)}, u32[]{:S(2)}) copy-start(f32[128]{0:T(128)} %param.21) | copy-start | bytes 1540
  108.8 43.6 %copy-start.27 = (f32[128]{0:T(128)S(1)}, f32[128]{0:T(128)}, u32[]{:S(2)}) copy-start(f32[128]{0:T(128)} %param.20) | copy-start | bytes 1540
  198.0 40.9 %copy-start.4 = (bf16[1,16,512,128]{3,2,1,0:T(8,128)(2,1)}, bf16[1,16,512,128]{3,2,1,0:T(8,128)(2,1)S(1)}, u32[]{:S(2)}) copy-start(bf16[1,16,512,128]{3,2,1,0:T(8,128)(2,1)S(1)} %get-tuple-element.22) | copy-start | bytes 6291460
  210.7 10.5 %collective-permute-start.6 = (bf16[1,1,512,128]{3,2,1,0:T(8,128)(2,1)S(1)}, bf16[1,1,512,128]{3,2,1,0:T(8,128)(2,1)S(1)}, u32[]{:S(2)}, u32[]{:S(2)}) collective-permute-start(bf16[1,1,512,128]{3,2,1,0:T(8,128)(2,1)S(1)} %get-tuple-element.28), channel_id=1, source_target_pairs={{0,1},{1,2},{2,3},{3,4},{4,5},{5,6},{6,7},{8,9},{9,10},{10,11},{11... | collective-permute-start | bytes 393224 | tf_op jit(solution)/shard_map/ppermute | solution.py:19
  212.0 9.2 %collective-permute-start.7 = (bf16[1,1,512,128]{3,2,1,0:T(8,128)(2,1)S(1)}, bf16[1,1,512,128]{3,2,1,0:T(8,128)(2,1)S(1)}, u32[]{:S(2)}, u32[]{:S(2)}) collective-permute-start(bf16[1,1,512,128]{3,2,1,0:T(8,128)(2,1)S(1)} %get-tuple-element.27), channel_id=1, source_target_pairs={{1,0},{2,1},{3,2},{4,3},{5,4},{6,5},{7,6},{9,8},{10,9},{11,10},{12... | collective-permute-start | bytes 393224 | tf_op jit(solution)/shard_map/ppermute | solution.py:22
  214.1 51.6 %collective-permute-start.9 = (bf16[1,1,512,128]{3,2,1,0:T(8,128)(2,1)}, bf16[1,1,512,128]{3,2,1,0:T(8,128)(2,1)S(1)}, u32[]{:S(2)}, u32[]{:S(2)}) collective-permute-start(bf16[1,1,512,128]{3,2,1,0:T(8,128)(2,1)} %get-tuple-element.26), channel_id=1, source_target_pairs={{1,0},{2,1},{3,2},{4,3},{5,4},{6,5},{7,6},{9,8},{10,9},{11,10},{12... | collective-permute-start | bytes 393224 | tf_op jit(solution)/shard_map/ppermute | solution.py:22
  215.4 50.3 %collective-permute-start.8 = (bf16[1,1,512,128]{3,2,1,0:T(8,128)(2,1)}, bf16[1,1,512,128]{3,2,1,0:T(8,128)(2,1)}, u32[]{:S(2)}, u32[]{:S(2)}) collective-permute-start(bf16[1,1,512,128]{3,2,1,0:T(8,128)(2,1)} %get-tuple-element.25), channel_id=1, source_target_pairs={{0,1},{1,2},{2,3},{3,4},{4,5},{5,6},{6,7},{8,9},{9,10},{10,11},{11... | collective-permute-start | bytes 393224 | tf_op jit(solution)/shard_map/ppermute | solution.py:19
  254.1 102.4 %copy-start.5 = (bf16[16,512,128]{2,1,0:T(8,128)(2,1)}, bf16[16,512,128]{2,1,0:T(8,128)(2,1)S(1)}, u32[]{:S(2)}) copy-start(bf16[16,512,128]{2,1,0:T(8,128)(2,1)S(1)} %fusion.10) | copy-start | bytes 6291460
  265.6 188.6 %all-reduce.11.cloned.1.call-start = ((), (), s32[]{:S(2)}) async-start(), calls=%async_computation.2 | async-start | bytes 147456 | tf_op jit(solution)/shard_map/psum | solution.py:189
  346.9 5.3 %collective-permute-start.10 = (bf16[1,1,512,128]{3,2,1,0:T(8,128)(2,1)S(1)}, bf16[1,1,512,128]{3,2,1,0:T(8,128)(2,1)S(1)}, u32[]{:S(2)}, u32[]{:S(2)}) collective-permute-start(bf16[1,1,512,128]{3,2,1,0:T(8,128)(2,1)S(1)} %get-tuple-element.24), channel_id=1, source_target_pairs={{0,1},{1,2},{2,3},{3,4},{4,5},{5,6},{6,7},{8,9},{9,10},{10,11},{11... | collective-permute-start | bytes 393224 | tf_op jit(solution)/shard_map/ppermute | solution.py:19
  349.6 6.9 %collective-permute-start.11 = (bf16[1,1,512,128]{3,2,1,0:T(8,128)(2,1)S(1)}, bf16[1,1,512,128]{3,2,1,0:T(8,128)(2,1)S(1)}, u32[]{:S(2)}, u32[]{:S(2)}) collective-permute-start(bf16[1,1,512,128]{3,2,1,0:T(8,128)(2,1)S(1)} %get-tuple-element.23), channel_id=1, source_target_pairs={{1,0},{2,1},{3,2},{4,3},{5,4},{6,5},{7,6},{9,8},{10,9},{11,10},{12... | collective-permute-start | bytes 393224 | tf_op jit(solution)/shard_map/ppermute | solution.py:22
  (19 other events, 119.9 us)
Sparse Core Ops, SparseCore 0:
  265.7 68.3 reduce-scatter.1
  375.4 78.7 all-reduce.10
where the time goes:
time: 471 us; the launch traced here: 463 us
  matrix products  192 us (41%)
  blocking collectives  126 us (27%)
  waiting for transfers between devices  66.5 us (14%)
  starting transfers between devices  31.3 us (7%)
  other arithmetic  25.7 us (5%)
  between operations  17.1 us (4%)
    psum x1, blocking collectives, shards(): lax.psum((gain_term, bias_term, image_weight), ('dp', 'slab'))  72 us
    dot_general x18, matrix products, data_grad(): total = total + jnp.dot(piece, block.T, preferred_element_type=jnp.float32)  70.1 us
    psum x1, waiting for transfers between devices, shards(): slab_total = lax.psum(stacked, 'slab')  64.1 us
    dot_general x18, matrix products, conv_rows(): total = total + jnp.dot(piece, block, preferred_element_type=jnp.float32)  60.4 us
    dot_general x9, matrix products, shards(): lax.dot_general(back_piece, block, (((1,), (0,)), ((), ())), preferred_el...  40.4 us
    psum x1, blocking collectives, shards(): lax.psum((group_sum(masked), group_sum(masked * hidden_two)), 'slab')  29.7 us
    psum x1, blocking collectives, shards(): lax.psum((group_sum(grad_normed), group_sum(grad_normed * normed)), 'slab')  24.1 us
    ppermute x6, starting transfers between devices, padded_2(): lax.ppermute(lax.slice_in_dim(block, block.shape[dim] - width, None, axis...  23.5 us
  transfers between devices with their start and end apart: 14, of which 3 were waited for; matrix products, arithmetic and copies ran while one was open for 26% of the time, Pallas kernels for 0%

commit v1 on v0

v1 whole, which is shorter than its diff:
```python
import functools
import math

import jax
import jax.numpy as jnp
from jax import lax
from jax.experimental import pallas as pl
from jax.experimental.pallas import tpu as pltpu
from jax.sharding import PartitionSpec as P

MESH = pl.DeviceIdType.MESH
F32 = jnp.float32
BF16 = jnp.bfloat16
PER_GROUP = 4
NORM_EPS = 1e-06
S = 16
C = 128


def dot(a, b):
    return jnp.dot(a, b, preferred_element_type=F32)


def sigmoid(v):
    return 0.5 * jnp.tanh(0.5 * v) + 0.5


def group_total(v):
    lane = lax.broadcasted_iota(jnp.int32, v.shape, 1)
    v = v + jnp.where(lane % 2 == 0, pltpu.roll(v, C - 1, 1), pltpu.roll(v, 1, 1))
    return v + jnp.where(lane % 4 < 2, pltpu.roll(v, C - 2, 1), pltpu.roll(v, 2, 1))


def kernel(
    ndp, nslab, rows, width, pixel_scale,
    lat_ref, img_ref, h_ref, w_ref, bk_ref, bs_ref, w1_ref, w2_ref, ci_ref, gain_ref, bias_ref,
    gw1_ref, gw2_ref, gci_ref, gg_ref, gb_ref, gl_ref,
    perm, permt, col, latp, act, mid, actt, midt, h1, h2, gs, nact, b2, b1,
    w4, ci4f, ci4, gstage, gimg, acc, flat, imgacc, sums, stat_send, stat_recv,
    send_a, recv_a, send_b, recv_b, small_a, small_ra, small_b, small_rb,
    halo_s, halo_r, stat_ss, stat_rs, a_ss, a_rs, b_ss, b_rs,
):
    t_count = width // S
    last = rows + 1
    npair = rows // 2
    blk = (9 * C) // ndp
    dp = lax.axis_index("dp")
    slab = lax.axis_index("slab")

    barrier = pltpu.get_barrier_semaphore()

    def greet(axis, me, n):
        def body(off, _):
            pl.semaphore_signal(
                barrier, inc=1, device_id={axis: lax.rem(me + off, n)}, device_id_type=MESH
            )
            return 0
        lax.fori_loop(1, n, body, 0)

    greet("slab", slab, nslab)
    greet("dp", dp, ndp)

    height = h_ref[0]
    limit = w_ref[0]
    count = (height * limit * PER_GROUP).astype(F32)

    def inside(r):
        return col[...] < jnp.where(slab * rows + r < height, limit, 0)

    def loop(lo, hi, body):
        def step(i, _):
            body(i)
            return 0
        lax.fori_loop(lo, hi, step, 0)

    def put(ref, row, a):
        ref[row, 1:t_count + 1] = a.reshape(t_count, S, C)
        sub = lax.broadcasted_iota(jnp.int32, (S, C), 0)
        low = pltpu.roll(a[width - S:].astype(F32), 1, 0)
        ref[row, 0] = jnp.where(sub == 0, 0.0, low).astype(BF16)
        high = pltpu.roll(a[:S].astype(F32), S - 1, 0)
        ref[row, t_count + 1] = jnp.where(sub == S - 1, 0.0, high).astype(BF16)

    def halo(ref, e, d):
        if d == 0:
            src, dst, to = 1, last, lax.rem(slab + nslab - 1, nslab)
        else:
            src, dst, to = last - 1, 0, lax.rem(slab + 1, nslab)
        return pltpu.make_async_remote_copy(
            src_ref=ref.at[src], dst_ref=ref.at[dst],
            send_sem=halo_s.at[e, d], recv_sem=halo_r.at[e, d],
            device_id={"slab": to}, device_id_type=MESH,
        )

    def halo_start(ref, e):
        for d in range(2):
            halo(ref, e, d).start()

    def halo_wait(ref, e):
        for d in range(2):
            halo(ref, e, d).wait()

        @pl.when(slab == 0)
        def _():
            ref[0] = jnp.zeros(ref.shape[1:], ref.dtype)

        @pl.when(slab == nslab - 1)
        def _():
            ref[last] = jnp.zeros(ref.shape[1:], ref.dtype)

    def spread(src_of, recv, ss, rs, e, axis, me, n):
        def copy(peer, slot):
            return pltpu.make_async_remote_copy(
                src_ref=src_of(peer), dst_ref=recv.at[slot],
                send_sem=ss.at[e, peer], recv_sem=rs.at[e, slot],
                device_id={axis: peer}, device_id_type=MESH,
            )

        def start():
            def body(off):
                copy(lax.rem(me + off, n), me).start()
            loop(1, n, body)

        def wait():
            def body(off):
                peer = lax.rem(me + off, n)
                copy(peer, peer).wait_recv()
                copy(peer, me).wait_send()
            loop(1, n, body)

        return start, wait

    a_i = lax.broadcasted_iota(jnp.int32, (width, width), 0)
    b_i = lax.broadcasted_iota(jnp.int32, (width, width), 1)
    perm[...] = jnp.where((a_i % S) * t_count + a_i // S == b_i, 1.0, 0.0).astype(BF16)
    permt[...] = jnp.where((b_i % S) * t_count + b_i // S == a_i, 1.0, 0.0).astype(BF16)
    j_i = lax.broadcasted_iota(jnp.int32, (width, C), 0)
    col[...] = (j_i % S) * t_count + j_i // S

    def stage_input(i):
        x = dot(perm[...], jnp.concatenate([lat_ref[2 * i], lat_ref[2 * i + 1]], axis=1))
        for k in range(2):
            r = 2 * i + k
            v = x[:, k * C:(k + 1) * C]
            latp[r] = v.astype(BF16)
            a = jnp.where(inside(r), v * sigmoid(v), 0.0).astype(BF16)
            put(act, r + 1, a)
            actt[r + 1] = a.T

    loop(0, npair, stage_input)

    scale = bs_ref[bk_ref[0]]
    row3 = lax.broadcasted_iota(jnp.int32, (3, rows, width), 1) + slab * rows
    lane3 = lax.broadcasted_iota(jnp.int32, (3, rows, width), 2)
    graded = jnp.where((row3 < height) & (lane3 < limit), img_ref[...].astype(F32) * scale, 0.0)
    graded = graded.reshape(3 * rows, width)
    lane = lax.broadcasted_iota(jnp.int32, (3 * rows, width), 1)
    shifted = [
        jnp.where(lane == width - 1, 0.0, pltpu.roll(graded, width - 1, 1)),
        graded,
        jnp.where(lane == 0, 0.0, pltpu.roll(graded, 1, 1)),
    ]
    stacked = jnp.concatenate([s.astype(BF16) for s in shifted], axis=0)
    gstage[...] = jnp.zeros_like(gstage)
    placed = dot(stacked, permt[...])
    for k in range(width // C):
        gstage[k, 0:9 * rows] = placed[:, k * C:(k + 1) * C]
        for r in range(rows):
            gimg[r + 1, :, k * C:(k + 1) * C] = gstage[k, pl.ds(r, 16, stride=rows), :].astype(BF16)

    pl.semaphore_wait(barrier, ndp + nslab - 2)
    halo_start(act, 0)
    halo_start(gimg, 1)

    for c, (ref, flip) in enumerate(((w1_ref, False), (w2_ref, False), (w2_ref, True), (w1_ref, True))):
        for j in range(4):
            for q in range(3):
                at = (j * 3 + q) * C
                for k in range(2):
                    if 0 <= j - k <= 2:
                        tap = 3 * (j - k) + q
                        if flip:
                            b = ref[(8 - tap) * C:(9 - tap) * C, :].T
                        else:
                            b = ref[tap * C:(tap + 1) * C, :]
                    else:
                        b = jnp.zeros((C, C), BF16)
                    w4[c, at:at + C, k * C:(k + 1) * C] = b
    ci4f[...] = jnp.zeros_like(ci4f)
    for p in range(3):
        for q in range(3):
            piece = ci_ref[:, (3 * p + q) * C:(3 * p + q + 1) * C].astype(F32)
            for k in range(2):
                at = (2 - p + k) * 16 + q * 3
                ci4f[at:at + 3, k * C:(k + 1) * C] = piece
    ci4[...] = ci4f[...].astype(BF16)

    def conv(src, c, i):
        taps = [
            src[2 * i + j, q:q + t_count].reshape(width, C) for j in range(4) for q in range(3)
        ]
        return dot(jnp.concatenate(taps, axis=1), w4[c])

    def ends(body):
        loop(0, 2, lambda k: body(k * (npair - 1)))

    def stage_one(i):
        y = conv(act, 0, i)
        for k in range(2):
            r = 2 * i + k
            hb = y[:, k * C:(k + 1) * C].astype(BF16)
            h1[r] = hb
            hf = hb.astype(F32)
            m = jnp.where(inside(r), hf * sigmoid(hf), 0.0).astype(BF16)
            put(mid, r + 1, m)
            midt[r + 1] = m.T

    loop(1, npair - 1, stage_one)
    halo_wait(act, 0)
    ends(stage_one)
    halo_start(mid, 2)
    for e in (0, last):
        actt[e] = act[e, 1:t_count + 1].reshape(width, C).T

    sums[...] = jnp.zeros_like(sums)

    def fold(v):
        return jnp.sum(v.reshape(width // 8, 8, C), axis=0)

    def stage_two(i):
        y = conv(mid, 1, i)
        for k in range(2):
            r = 2 * i + k
            v = y[:, k * C:(k + 1) * C] + latp[r].astype(F32)
            h2[r] = v
            masked = jnp.where(inside(r), v, 0.0)
            sums[0] += fold(masked)
            sums[1] += fold(masked * v)

    loop(1, npair - 1, stage_two)
    halo_wait(mid, 2)
    ends(stage_two)

    def stats(e):
        stat_send[e, 0:1] = jnp.sum(sums[2 * e], axis=0, keepdims=True)
        stat_send[e, 1:2] = jnp.sum(sums[2 * e + 1], axis=0, keepdims=True)
        stat_recv[e, slab] = stat_send[e]
        return spread(
            lambda peer: stat_send.at[e], stat_recv.at[e], stat_ss, stat_rs, e, "slab", slab, nslab
        )

    def stat_total(e):
        total = stat_recv[e, 0]
        for k in range(1, nslab):
            total = total + stat_recv[e, k]
        return total

    for e in range(2):
        stat_send[e] = jnp.zeros(stat_send.shape[1:], F32)
    start, wait = stats(0)
    start()

    halo_wait(gimg, 1)

    def stage_image(i):
        y = lax.dot_general(
            gimg[pl.ds(2 * i, 4)].reshape(64, width), ci4[...], (((0,), (0,)), ((), ())),
            preferred_element_type=F32,
        )
        for k in range(2):
            gs[2 * i + k] = y[:, k * C:(k + 1) * C]

    loop(0, npair, stage_image)
    for e in (0, last):
        midt[e] = mid[e, 1:t_count + 1].reshape(width, C).T
    wait()

    total = stat_total(0)
    mean = group_total(total[0:1]) / count
    rstd = lax.rsqrt(group_total(total[1:2]) / count - mean * mean + NORM_EPS)
    gain = gain_ref[...]
    bias = bias_ref[...]

    def stage_norm(r):
        n = (h2[r] - mean) * rstd
        v = n * gain + bias
        s = sigmoid(v)
        vs = v * s
        here = inside(r)
        nact[r] = jnp.where(here, vs, 0.0).astype(BF16)
        g = jnp.where(here, gs[r] * (s + vs * (1.0 - s)), 0.0)
        h2[r] = n
        gs[r] = g
        sums[2] += fold(g)
        sums[3] += fold(g * n)

    loop(0, rows, stage_norm)
    start, wait = stats(1)
    start()

    imgacc[...] = jnp.zeros_like(imgacc)

    def stage_imgw(i):
        imgacc[...] += dot(
            gimg[pl.ds(2 * i, 4)].reshape(64, width),
            jnp.concatenate([nact[2 * i], nact[2 * i + 1]], axis=1),
        )

    loop(0, npair, stage_imgw)
    small_a[...] = imgacc[0:48, 0:C] + imgacc[16:64, C:2 * C]
    small_a[9:11] = jnp.concatenate(
        [jnp.sum(sums[3], axis=0, keepdims=True), jnp.sum(sums[2], axis=0, keepdims=True)], axis=0
    )
    small_ra[dp] = small_a[...]
    small_start, small_wait = spread(
        lambda peer: small_a, small_ra, a_ss, a_rs, 0, "dp", dp, ndp
    )
    wait()
    small_start()

    total = stat_total(1)
    c1 = rstd * gain
    c0 = rstd * (group_total(total[0:1] * gain) / count)
    c2 = rstd * (group_total(total[1:2] * gain) / count)

    def stage_grad_two(r):
        g = jnp.where(inside(r), gs[r] * c1 - c0 - h2[r] * c2, 0.0).astype(BF16)
        put(b2, r + 1, g)

    loop(0, 2, lambda k: stage_grad_two(k * (rows - 1)))
    halo_start(b2, 3)
    loop(1, rows - 1, stage_grad_two)

    def weight_grad(at, b):
        acc[...] = jnp.zeros_like(acc)

        def piece(row, q):
            return b[row, 2 - q:2 - q + t_count].reshape(width, C)

        def body(i):
            lhs = jnp.concatenate(
                [at[pl.ds(2 * i + k, 3)].reshape(3 * C, width) for k in range(2)], axis=1
            )
            rhs = jnp.concatenate(
                [
                    jnp.concatenate([piece(2 * i + 1 + k, q) for q in range(2)], axis=1)
                    for k in range(2)
                ],
                axis=0,
            )
            acc[:, 0:2 * C] += dot(lhs, rhs)
            rhs = jnp.concatenate([piece(2 * i + 1 + k, 2) for k in range(2)], axis=1)
            z = dot(at[pl.ds(2 * i, 4)].reshape(4 * C, width), rhs)
            acc[:, 2 * C:] += z[0:3 * C, 0:C] + z[C:, C:]

        loop(0, npair, body)

    def scatter(e):
        for p in range(3):
            for q in range(3):
                flat[(3 * p + q) * C:(3 * p + q + 1) * C] = acc[p * C:(p + 1) * C, q * C:(q + 1) * C]

        def body(d):
            send_a[e, d, 0:blk] = flat[pl.ds(pl.multiple_of(d * blk, 8), blk)].astype(BF16)
        loop(0, ndp, body)
        recv_a[e, dp] = send_a[e, dp]
        return spread(
            lambda peer: send_a.at[e, peer], recv_a.at[e], a_ss, a_rs, 1 + e, "dp", dp, ndp
        )

    def gather(e):
        part = recv_a[e, 0].astype(F32)
        for k in range(1, ndp):
            part = part + recv_a[e, k].astype(F32)
        send_b[e] = part.astype(BF16)
        recv_b[e, slab] = send_b[e]
        return spread(lambda peer: send_b.at[e], recv_b.at[e], b_ss, b_rs, 1 + e, "slab", slab, nslab)

    def finish(e, out):
        part = recv_b[e, 0].astype(F32)
        for k in range(1, nslab):
            part = part + recv_b[e, k].astype(F32)
        out[...] = part[0:blk] * pixel_scale

    send_a[...] = jnp.zeros_like(send_a)
    weight_grad(midt, b2)
    second_start, second_wait = scatter(0)
    second_start()

    halo_wait(b2, 3)

    def stage_grad_one(i):
        y = conv(b2, 2, i)
        for k in range(2):
            r = 2 * i + k
            v = h1[r].astype(F32)
            s = sigmoid(v)
            slope = s + v * s * (1.0 - s)
            g = jnp.where(inside(r), y[:, k * C:(k + 1) * C] * slope, 0.0).astype(BF16)
            put(b1, r + 1, g)

    ends(stage_grad_one)
    halo_start(b1, 4)
    loop(1, npair - 1, stage_grad_one)

    small_wait()
    part = small_ra[0]
    for k in range(1, ndp):
        part = part + small_ra[k]
    small_b[...] = part
    small_rb[slab] = part
    small_b_start, small_b_wait = spread(
        lambda peer: small_b, small_rb, b_ss, b_rs, 0, "slab", slab, nslab
    )
    small_b_start()
    second_wait()
    second_b_start, second_b_wait = gather(0)
    second_b_start()

    weight_grad(actt, b1)
    first_start, first_wait = scatter(1)
    first_start()
    halo_wait(b1, 4)

    def stage_latents(i):
        y = conv(b1, 3, i)
        done = []
        for k in range(2):
            r = 2 * i + k
            v = latp[r].astype(F32)
            s = sigmoid(v)
            slope = s + v * s * (1.0 - s)
            g = jnp.where(inside(r), y[:, k * C:(k + 1) * C] * slope, 0.0)
            own = b2[r + 1, 1:t_count + 1].reshape(width, C).astype(F32)
            done.append((own + g).astype(BF16))
        z = dot(permt[...], jnp.concatenate(done, axis=1)).astype(BF16)
        for k in range(2):
            gl_ref[2 * i + k] = z[:, k * C:(k + 1) * C]

    half = npair * 3 // 4
    loop(0, half, stage_latents)
    first_wait()
    first_b_start, first_b_wait = gather(1)
    first_b_start()
    loop(half, npair, stage_latents)

    small_b_wait()
    part = small_rb[0]
    for k in range(1, nslab):
        part = part + small_rb[k]
    part = part * pixel_scale
    gg_ref[...] = part[9:10]
    gb_ref[...] = part[10:11]
    for p in range(3):
        for q in range(3):
            at = (2 - p) * 16 + q * 3
            gci_ref[:, (3 * p + q) * C:(3 * p + q + 1) * C] = part[at:at + 3]
    second_b_wait()
    finish(0, gw2_ref)
    first_b_wait()
    finish(1, gw1_ref)


def shards(
    latents, image_grad, heights, widths, buckets, bucket_scale,
    conv_first, conv_second, conv_image, norm_gain, norm_bias,
):
    images, rows, width, channels = latents.shape
    ndp = lax.axis_size("dp")
    nslab = lax.axis_size("slab")
    t_count = width // S
    pixel_scale = 1.0 / math.sqrt(images * ndp * rows * nslab * width)
    blk = 9 * C // ndp
    pad = -(-blk // 16) * 16
    vmem = pl.BlockSpec(memory_space=pltpu.VMEM)
    smem = pl.BlockSpec(memory_space=pltpu.SMEM)
    edge = (rows + 2, t_count + 2, S, C)
    scratch = [
        pltpu.VMEM((width, width), BF16),
        pltpu.VMEM((width, width), BF16),
        pltpu.VMEM((width, C), jnp.int32),
        pltpu.VMEM((rows, width, C), BF16),
        pltpu.VMEM(edge, BF16),
        pltpu.VMEM(edge, BF16),
        pltpu.VMEM((rows + 2, C, width), BF16),
        pltpu.VMEM((rows + 2, C, width), BF16),
        pltpu.VMEM((rows, width, C), BF16),
        pltpu.VMEM((rows, width, C), F32),
        pltpu.VMEM((rows, width, C), F32),
        pltpu.VMEM((rows, width, C), BF16),
        pltpu.VMEM(edge, BF16),
        pltpu.VMEM(edge, BF16),
        pltpu.VMEM((4, 12 * C, 2 * C), BF16),
        pltpu.VMEM((64, 2 * C), F32),
        pltpu.VMEM((64, 2 * C), BF16),
        pltpu.VMEM((width // C, 16 * rows, C), F32),
        pltpu.VMEM((rows + 2, 16, width), BF16),
        pltpu.VMEM((3 * C, 3 * C), F32),
        pltpu.VMEM((9 * C, C), F32),
        pltpu.VMEM((64, 2 * C), F32),
        pltpu.VMEM((4, 8, C), F32),
        pltpu.VMEM((2, 8, C), F32),
        pltpu.VMEM((2, nslab, 8, C), F32),
        pltpu.VMEM((2, ndp, pad, C), BF16),
        pltpu.VMEM((2, ndp, pad, C), BF16),
        pltpu.VMEM((2, pad, C), BF16),
        pltpu.VMEM((2, nslab, pad, C), BF16),
        pltpu.VMEM((48, C), F32),
        pltpu.VMEM((ndp, 48, C), F32),
        pltpu.VMEM((48, C), F32),
        pltpu.VMEM((nslab, 48, C), F32),
        pltpu.SemaphoreType.DMA((5, 2)),
        pltpu.SemaphoreType.DMA((5, 2)),
        pltpu.SemaphoreType.DMA((2, nslab)),
        pltpu.SemaphoreType.DMA((2, nslab)),
        pltpu.SemaphoreType.DMA((3, ndp)),
        pltpu.SemaphoreType.DMA((3, ndp)),
        pltpu.SemaphoreType.DMA((3, nslab)),
        pltpu.SemaphoreType.DMA((3, nslab)),
    ]
    gw1, gw2, gci, gg, gb, gl = pl.pallas_call(
        functools.partial(kernel, ndp, nslab, rows, width, pixel_scale),
        out_shape=(
            jax.ShapeDtypeStruct((blk, C), F32),
            jax.ShapeDtypeStruct((blk, C), F32),
            jax.ShapeDtypeStruct((3, 9 * C), F32),
            jax.ShapeDtypeStruct((1, C), F32),
            jax.ShapeDtypeStruct((1, C), F32),
            jax.ShapeDtypeStruct((rows, width, C), BF16),
        ),
        in_specs=[vmem, vmem, smem, smem, smem, smem, vmem, vmem, vmem, vmem, vmem],
        out_specs=(vmem,) * 6,
        scratch_shapes=scratch,
        compiler_params=pltpu.CompilerParams(
            collective_id=0, has_side_effects=True, vmem_limit_bytes=60 * 2**20
        ),
        cost_estimate=pl.CostEstimate(
            flops=int(1.6e10), bytes_accessed=5 * 2**20, transcendentals=5 * 2**20
        ),
    )(
        latents[0], image_grad[0], heights, widths, buckets, bucket_scale,
        conv_first, conv_second, conv_image, norm_gain[None], norm_bias[None],
    )
    return gw1, gw2, gci, gg[0], gb[0], gl[None]


def solution(mesh):
    placed = (
        P("dp", "slab", None, None),
        P("dp", None, "slab", None),
        P("dp"),
        P("dp"),
        P("dp"),
        P(),
        P(),
        P(),
        P(),
        P(),
        P(),
    )
    return jax.shard_map(
        shards,
        mesh=mesh,
        in_specs=placed,
        out_specs=(P("dp", None), P("dp", None), P(), P(), P(), P("dp", "slab", None, None)),
        check_vma=False,
    )
```

time: 471 us -> 85 us (0.18); the launches traced: 463 us -> 83.5 us
  matrix products: 192 us -> 0 us
  blocking collectives: 126 us -> 0 us
  Pallas kernels: 0 us -> 71.3 us
  waiting for transfers between devices: 66.5 us -> 0 us
  starting transfers between devices: 31.3 us -> 0 us
  other arithmetic: 25.7 us -> 0 us
  between operations: 17.1 us -> 2.58 us
  local copies, waits for them, and re-layouts: 4.5 us -> 9.56 us
    dot_general x72 -> x0, matrix products: 192 us -> none  [the longest x18 70.1 us: data_grad(): total = total + jnp.dot(piece, block.T, preferred_element_type=jnp.float32)]
    psum x3 -> x0, blocking collectives: 126 us -> none  [the longest x1 72 us: shards(): lax.psum((gain_term, bias_term, image_weight), ('dp', 'slab'))]
    pallas_call x0 -> x1, Pallas kernels: none -> 71.3 us  [shards(): pl.pallas_call(functools.partial(kernel, ndp, nslab, rows, width, pixel_s...]
    psum x1 -> x0, waiting for transfers between devices: 64.1 us -> none  [shards(): slab_total = lax.psum(stacked, 'slab')]
    ppermute x12 -> x0, starting transfers between devices: 31.3 us -> none  [the longest x6 23.5 us: padded_2(): lax.ppermute(lax.slice_in_dim(block, block.shape[dim] - width, None, axis...]
    convert_element_type x5 -> x0, other arithmetic: 10.7 us -> none  [the longest x3 9.89 us: silu_mask(): (jax.nn.silu(value.astype(jnp.float32)) * inside[..., None]).astype(jnp.b...]
    concatenate x6 -> x0, other arithmetic: 10.2 us -> none  [padded_2(): block = jnp.concatenate([low, block, high], axis=dim)]
    unnamed x58 -> x6, local copies, waits for them, and re-layouts: 1.93 us -> 9.56 us
  transfers between devices with their start and end apart: 14 -> 0, of which waited for: 3 -> 0; matrix products, arithmetic and copies ran while one was open for 26% -> 0% of each run, Pallas kernels for 0% -> 0%
where the time goes in v1:
time: 85 us; the launch traced here: 83.5 us
  Pallas kernels  71.3 us (84%)
  local copies, waits for them, and re-layouts  9.56 us (11%)
  between operations  2.58 us (3%)
    pallas_call x1, Pallas kernels, shards(): pl.pallas_call(functools.partial(kernel, ndp, nslab, rows, width, pixel_s...  71.3 us
    unnamed x6, local copies, waits for them, and re-layouts  9.56 us

profile of v1, /device:TPU:0, one launch (start us, length us, event | category | flops | bytes accessed | tf_op | source)
XLA Modules:
  0.0 83.5 jit_solution(9891320584293345925)
XLA Ops:
  2.6 71.3 %shard_map.154 = (f32[72,128]{1,0:T(8,128)}, f32[72,128]{1,0:T(8,128)}, f32[3,1152]{1,0:T(4,128)}, f32[1,128]{1,0:T(1,128)}, f32[1,128]{1,0:T(1,128)}, /*index=5*/bf16[16,512,128]{2,1,0:T(8,128)(2,1)}) custom-call(bf16[16,512,128]{2,1,0:T(8,128)(2,1)} %bitcast.8, bf16[3,16,512]{2,1,0:T(8,128)(2,1)} %bitcast.9, s32[1]{0:T(128)S(6)} %copy.23.h_ref, ...), custom_call_target="tpu_custom_call" | custom-call | flops 16000000000 | bytes 5242880 | tf_op jit(solution)/shard_map/pallas_call | solution.py:521
  73.9 1.4 %copy.26 = f32[72,128]{1,0:T(8,128)} copy(f32[72,128]{1,0:T(8,128)} %get-tuple-element.24) | data formatting | bytes 73728
  75.3 1.4 %copy.27 = f32[72,128]{1,0:T(8,128)} copy(f32[72,128]{1,0:T(8,128)} %get-tuple-element.25) | data formatting | bytes 73728
  76.7 1.3 %copy.28 = f32[3,1152]{1,0:T(4,128)} copy(f32[3,1152]{1,0:T(4,128)} %get-tuple-element.26) | data formatting | bytes 27648
  78.0 1.2 %copy.29 = f32[128]{0:T(128)} copy(f32[128]{0:T(128)} %bitcast.13) | data formatting | bytes 1024
  79.2 1.2 %copy.30 = f32[128]{0:T(128)} copy(f32[128]{0:T(128)} %bitcast.12) | data formatting | bytes 1024
  80.4 3.1 %copy.31 = bf16[1,16,512,128]{3,2,1,0:T(8,128)(2,1)} copy(bf16[1,16,512,128]{3,2,1,0:T(8,128)(2,1)} %bitcast.7) | data formatting | bytes 4194304

commit v2 on v1

--- a/solution.py
+++ b/solution.py
@@ -34,18 +34,34 @@
 def kernel(
     ndp, nslab, rows, width, pixel_scale,
     lat_ref, img_ref, h_ref, w_ref, bk_ref, bs_ref, w1_ref, w2_ref, ci_ref, gain_ref, bias_ref,
-    gw1_ref, gw2_ref, gci_ref, gg_ref, gb_ref, gl_ref,
-    perm, permt, col, latp, act, mid, actt, midt, h1, h2, gs, nact, b2, b1,
+    out_ref, pack_ref,
+    lat, glp, perm, permt, col, latp, act, mid, actt, midt, h1, h2, gs, nact, b2, b1,
     w4, ci4f, ci4, gstage, gimg, acc, flat, imgacc, sums, stat_send, stat_recv,
-    send_a, recv_a, send_b, recv_b, small_a, small_ra, small_b, small_rb,
-    halo_s, halo_r, stat_ss, stat_rs, a_ss, a_rs, b_ss, b_rs,
+    send_c, recv_c, send_a, recv_a, send_b, recv_b,
+    small_c, small_rc, small_a, small_ra, small_b, small_rb,
+    io_sem, halo_s, halo_r, stat_ss, stat_rs, c_ss, c_rs, a_ss, a_rs, b_ss, b_rs,
 ):
     t_count = width // S
     last = rows + 1
     npair = rows // 2
     blk = (9 * C) // ndp
+    nchip = ndp // 2
     dp = lax.axis_index("dp")
     slab = lax.axis_index("slab")
+    core = lax.rem(dp, 2)
+    chip = dp // 2
+
+    def latents_in(i):
+        part = pl.ds(2 * i, 2)
+        return pltpu.make_async_copy(lat_ref.at[part], lat.at[part], io_sem.at[0, i])
+
+    def latents_out(i):
+        part = pl.ds(2 * i, 2)
+        return pltpu.make_async_copy(glp.at[part], out_ref.at[part], io_sem.at[1, i])
+
+    latents_in(0).start()
+    latents_in(npair - 1).start()
+    lax.fori_loop(1, npair - 1, lambda i, _: (latents_in(i).start(), 0)[1], 0)
 
     barrier = pltpu.get_barrier_semaphore()
 
@@ -108,12 +124,12 @@
         def _():
             ref[last] = jnp.zeros(ref.shape[1:], ref.dtype)
 
-    def spread(src_of, recv, ss, rs, e, axis, me, n):
+    def spread(src_of, recv, ss, rs, e, axis, me, n, target=lambda peer: peer):
         def copy(peer, slot):
             return pltpu.make_async_remote_copy(
                 src_ref=src_of(peer), dst_ref=recv.at[slot],
                 send_sem=ss.at[e, peer], recv_sem=rs.at[e, slot],
-                device_id={axis: peer}, device_id_type=MESH,
+                device_id={axis: target(peer)}, device_id_type=MESH,
             )
 
         def start():
@@ -130,6 +146,17 @@
 
         return start, wait
 
+    def to_core(src, recv, e):
+        return pltpu.make_async_remote_copy(
+            src_ref=src, dst_ref=recv, send_sem=c_ss.at[e], recv_sem=c_rs.at[e],
+            device_id={"dp": dp + 1 - 2 * core}, device_id_type=MESH,
+        )
+
+    def to_chips(src_of, recv, e):
+        return spread(
+            src_of, recv, a_ss, a_rs, e, "dp", chip, nchip, lambda peer: 2 * peer + core
+        )
+
     a_i = lax.broadcasted_iota(jnp.int32, (width, width), 0)
     b_i = lax.broadcasted_iota(jnp.int32, (width, width), 1)
     perm[...] = jnp.where((a_i % S) * t_count + a_i // S == b_i, 1.0, 0.0).astype(BF16)
@@ -137,8 +164,12 @@
     j_i = lax.broadcasted_iota(jnp.int32, (width, C), 0)
     col[...] = (j_i % S) * t_count + j_i // S
 
+    def ends(body):
+        loop(0, 2, lambda k: body(k * (npair - 1)))
+
     def stage_input(i):
-        x = dot(perm[...], jnp.concatenate([lat_ref[2 * i], lat_ref[2 * i + 1]], axis=1))
+        latents_in(i).wait()
+        x = dot(perm[...], jnp.concatenate([lat[2 * i], lat[2 * i + 1]], axis=1))
         for k in range(2):
             r = 2 * i + k
             v = x[:, k * C:(k + 1) * C]
@@ -147,7 +178,10 @@
             put(act, r + 1, a)
             actt[r + 1] = a.T
 
-    loop(0, npair, stage_input)
+    ends(stage_input)
+    pl.semaphore_wait(barrier, ndp + nslab - 2)
+    halo_start(act, 0)
+    loop(1, npair - 1, stage_input)
 
     scale = bs_ref[bk_ref[0]]
     row3 = lax.broadcasted_iota(jnp.int32, (3, rows, width), 1) + slab * rows
@@ -168,8 +202,6 @@
         for r in range(rows):
             gimg[r + 1, :, k * C:(k + 1) * C] = gstage[k, pl.ds(r, 16, stride=rows), :].astype(BF16)
 
-    pl.semaphore_wait(barrier, ndp + nslab - 2)
-    halo_start(act, 0)
     halo_start(gimg, 1)
 
     for c, (ref, flip) in enumerate(((w1_ref, False), (w2_ref, False), (w2_ref, True), (w1_ref, True))):
@@ -201,9 +233,6 @@
         ]
         return dot(jnp.concatenate(taps, axis=1), w4[c])
 
-    def ends(body):
-        loop(0, 2, lambda k: body(k * (npair - 1)))
-
     def stage_one(i):
         y = conv(act, 0, i)
         for k in range(2):
@@ -215,10 +244,11 @@
             put(mid, r + 1, m)
             midt[r + 1] = m.T
 
-    loop(1, npair - 1, stage_one)
+    loop(1, npair // 2, stage_one)
     halo_wait(act, 0)
     ends(stage_one)
     halo_start(mid, 2)
+    loop(npair // 2, npair - 1, stage_one)
     for e in (0, last):
         actt[e] = act[e, 1:t_count + 1].reshape(width, C).T
 
@@ -307,16 +337,12 @@
         )
 
     loop(0, npair, stage_imgw)
-    small_a[...] = imgacc[0:48, 0:C] + imgacc[16:64, C:2 * C]
-    small_a[9:11] = jnp.concatenate(
-        [jnp.sum(sums[3], axis=0, keepdims=True), jnp.sum(sums[2], axis=0, keepdims=True)], axis=0
-    )
-    small_ra[dp] = small_a[...]
-    small_start, small_wait = spread(
-        lambda peer: small_a, small_ra, a_ss, a_rs, 0, "dp", dp, ndp
-    )
+    flat[0:48] = imgacc[0:48, 0:C] + imgacc[16:64, C:2 * C]
+    flat[9:10] = jnp.sum(sums[3], axis=0, keepdims=True)
+    flat[10:11] = jnp.sum(sums[2], axis=0, keepdims=True)
+    small_c[...] = flat[0:48].astype(BF16)
+    to_core(small_c, small_rc, 0).start()
     wait()
-    small_start()
 
     total = stat_total(1)
     c1 = rstd * gain
@@ -361,31 +387,51 @@
                 flat[(3 * p + q) * C:(3 * p + q + 1) * C] = acc[p * C:(p + 1) * C, q * C:(q + 1) * C]
 
         def body(d):
-            send_a[e, d, 0:blk] = flat[pl.ds(pl.multiple_of(d * blk, 8), blk)].astype(BF16)
+            send_c[e, lax.rem(d, 2), d // 2, 0:blk] = flat[
+                pl.ds(pl.multiple_of(d * blk, 8), blk)
+            ].astype(BF16)
         loop(0, ndp, body)
-        recv_a[e, dp] = send_a[e, dp]
-        return spread(
-            lambda peer: send_a.at[e, peer], recv_a.at[e], a_ss, a_rs, 1 + e, "dp", dp, ndp
-        )
+        copy = to_core(send_c.at[e, 1 - core], recv_c.at[e], 1 + e)
+        copy.start()
+        return copy
+
+    def chips(e):
+        def body(k):
+            both = send_c[e, core, k].astype(F32) + recv_c[e, k].astype(F32)
+            send_a[e, k] = both.astype(BF16)
+        loop(0, nchip, body)
+        recv_a[e, chip] = send_a[e, chip]
+        start, wait = to_chips(lambda peer: send_a.at[e, peer], recv_a.at[e], 1 + e)
+        start()
+        return wait
 
     def gather(e):
         part = recv_a[e, 0].astype(F32)
-        for k in range(1, ndp):
+        for k in range(1, nchip):
             part = part + recv_a[e, k].astype(F32)
         send_b[e] = part.astype(BF16)
         recv_b[e, slab] = send_b[e]
-        return spread(lambda peer: send_b.at[e], recv_b.at[e], b_ss, b_rs, 1 + e, "slab", slab, nslab)
-
-    def finish(e, out):
+        start, wait = spread(
+            lambda peer: send_b.at[e], recv_b.at[e], b_ss, b_rs, 1 + e, "slab", slab, nslab
+        )
+        start()
+        return wait
+
+    def finish(e):
         part = recv_b[e, 0].astype(F32)
         for k in range(1, nslab):
             part = part + recv_b[e, k].astype(F32)
-        out[...] = part[0:blk] * pixel_scale
-
-    send_a[...] = jnp.zeros_like(send_a)
+        pack_ref[e * blk:(e + 1) * blk] = part[0:blk] * pixel_scale
+
+    send_c[...] = jnp.zeros_like(send_c)
     weight_grad(midt, b2)
-    second_start, second_wait = scatter(0)
-    second_start()
+    second = scatter(0)
+
+    to_core(small_c, small_rc, 0).wait()
+    small_a[...] = (small_c[...].astype(F32) + small_rc[...].astype(F32)).astype(BF16)
+    small_ra[chip] = small_a[...]
+    small_start, small_wait = to_chips(lambda peer: small_a, small_ra, 0)
+    small_start()
 
     halo_wait(b2, 3)
 
@@ -401,30 +447,29 @@
 
     ends(stage_grad_one)
     halo_start(b1, 4)
+    second.wait()
+    second_wait = chips(0)
     loop(1, npair - 1, stage_grad_one)
 
     small_wait()
-    part = small_ra[0]
-    for k in range(1, ndp):
-        part = part + small_ra[k]
-    small_b[...] = part
-    small_rb[slab] = part
+    part = small_ra[0].astype(F32)
+    for k in range(1, nchip):
+        part = part + small_ra[k].astype(F32)
+    small_b[...] = part.astype(BF16)
+    small_rb[slab] = small_b[...]
     small_b_start, small_b_wait = spread(
         lambda peer: small_b, small_rb, b_ss, b_rs, 0, "slab", slab, nslab
     )
     small_b_start()
     second_wait()
-    second_b_start, second_b_wait = gather(0)
-    second_b_start()
+    second_b_wait = gather(0)
 
     weight_grad(actt, b1)
-    first_start, first_wait = scatter(1)
-    first_start()
+    first = scatter(1)
     halo_wait(b1, 4)
 
     def stage_latents(i):
         y = conv(b1, 3, i)
-        done = []
         for k in range(2):
             r = 2 * i + k
             v = latp[r].astype(F32)
@@ -432,33 +477,51 @@
             slope = s + v * s * (1.0 - s)
             g = jnp.where(inside(r), y[:, k * C:(k + 1) * C] * slope, 0.0)
             own = b2[r + 1, 1:t_count + 1].reshape(width, C).astype(F32)
-            done.append((own + g).astype(BF16))
-        z = dot(permt[...], jnp.concatenate(done, axis=1)).astype(BF16)
+            glp[r] = (own + g).astype(BF16)
+        latents_out(i).start()
+
+    loop(0, npair // 4, stage_latents)
+    first.wait()
+    first_wait = chips(1)
+    loop(npair // 4, npair * 5 // 8, stage_latents)
+    first_wait()
+    first_b_wait = gather(1)
+    loop(npair * 5 // 8, npair, stage_latents)
+
+    small_b_wait()
+    part = small_rb[0].astype(F32)
+    for k in range(1, nslab):
+        part = part + small_rb[k].astype(F32)
+    pack_ref[2 * blk:2 * blk + 48] = part * pixel_scale
+    second_b_wait()
+    finish(0)
+    first_b_wait()
+    finish(1)
+    loop(0, npair, lambda i: latents_out(i).wait())
+
+
+def unload(blk, step_rows, width, glp_ref, pack_ref, gw1_ref, gw2_ref, gci_ref, gg_ref, gb_ref, gl_ref, permt):
+    t_count = width // S
+
+    @pl.when(pl.program_id(0) == 0)
+    def _():
+        a_i = lax.broadcasted_iota(jnp.int32, (width, width), 0)
+        b_i = lax.broadcasted_iota(jnp.int32, (width, width), 1)
+        permt[...] = jnp.where((b_i % S) * t_count + b_i // S == a_i, 1.0, 0.0).astype(BF16)
+        gw1_ref[...] = pack_ref[blk:2 * blk]
+        gw2_ref[...] = pack_ref[0:blk]
+        base = 2 * blk
+        gg_ref[...] = pack_ref[base + 9:base + 10]
+        gb_ref[...] = pack_ref[base + 10:base + 11]
+        for p in range(3):
+            for q in range(3):
+                at = base + (2 - p) * 16 + q * 3
+                gci_ref[:, (3 * p + q) * C:(3 * p + q + 1) * C] = pack_ref[at:at + 3]
+
+    for i in range(step_rows // 2):
+        z = dot(permt[...], jnp.concatenate([glp_ref[2 * i], glp_ref[2 * i + 1]], axis=1))
         for k in range(2):
-            gl_ref[2 * i + k] = z[:, k * C:(k + 1) * C]
-
-    half = npair * 3 // 4
-    loop(0, half, stage_latents)
-    first_wait()
-    first_b_start, first_b_wait = gather(1)
-    first_b_start()
-    loop(half, npair, stage_latents)
-
-    small_b_wait()
-    part = small_rb[0]
-    for k in range(1, nslab):
-        part = part + small_rb[k]
-    part = part * pixel_scale
-    gg_ref[...] = part[9:10]
-    gb_ref[...] = part[10:11]
-    for p in range(3):
-        for q in range(3):
-            at = (2 - p) * 16 + q * 3
-            gci_ref[:, (3 * p + q) * C:(3 * p + q + 1) * C] = part[at:at + 3]
-    second_b_wait()
-    finish(0, gw2_ref)
-    first_b_wait()
-    finish(1, gw1_ref)
+            gl_ref[2 * i + k] = z[:, k * C:(k + 1) * C].astype(BF16)
 
 
 def shards(
@@ -474,8 +537,11 @@
     pad = -(-blk // 16) * 16
     vmem = pl.BlockSpec(memory_space=pltpu.VMEM)
     smem = pl.BlockSpec(memory_space=pltpu.SMEM)
+    nchip = ndp // 2
     edge = (rows + 2, t_count + 2, S, C)
     scratch = [
+        pltpu.VMEM((rows, width, C), BF16),
+        pltpu.VMEM((rows, width, C), BF16),
         pltpu.VMEM((width, width), BF16),
         pltpu.VMEM((width, width), BF16),
         pltpu.VMEM((width, C), jnp.int32),
@@ -501,35 +567,39 @@
         pltpu.VMEM((4, 8, C), F32),
         pltpu.VMEM((2, 8, C), F32),
         pltpu.VMEM((2, nslab, 8, C), F32),
-        pltpu.VMEM((2, ndp, pad, C), BF16),
-        pltpu.VMEM((2, ndp, pad, C), BF16),
+        pltpu.VMEM((2, 2, nchip, pad, C), BF16),
+        pltpu.VMEM((2, nchip, pad, C), BF16),
+        pltpu.VMEM((2, nchip, pad, C), BF16),
+        pltpu.VMEM((2, nchip, pad, C), BF16),
         pltpu.VMEM((2, pad, C), BF16),
         pltpu.VMEM((2, nslab, pad, C), BF16),
-        pltpu.VMEM((48, C), F32),
-        pltpu.VMEM((ndp, 48, C), F32),
-        pltpu.VMEM((48, C), F32),
-        pltpu.VMEM((nslab, 48, C), F32),
+        pltpu.VMEM((48, C), BF16),
+        pltpu.VMEM((48, C), BF16),
+        pltpu.VMEM((48, C), BF16),
+        pltpu.VMEM((nchip, 48, C), BF16),
+        pltpu.VMEM((48, C), BF16),
+        pltpu.VMEM((nslab, 48, C), BF16),
+        pltpu.SemaphoreType.DMA((2, rows // 2)),
         pltpu.SemaphoreType.DMA((5, 2)),
         pltpu.SemaphoreType.DMA((5, 2)),
         pltpu.SemaphoreType.DMA((2, nslab)),
         pltpu.SemaphoreType.DMA((2, nslab)),
-        pltpu.SemaphoreType.DMA((3, ndp)),
-        pltpu.SemaphoreType.DMA((3, ndp)),
+        pltpu.SemaphoreType.DMA((3,)),
+        pltpu.SemaphoreType.DMA((3,)),
+        pltpu.SemaphoreType.DMA((3, nchip)),
+        pltpu.SemaphoreType.DMA((3, nchip)),
         pltpu.SemaphoreType.DMA((3, nslab)),
         pltpu.SemaphoreType.DMA((3, nslab)),
     ]
-    gw1, gw2, gci, gg, gb, gl = pl.pallas_call(
+    anywhere = pl.BlockSpec(memory_space=pl.ANY)
+    glp, pack = pl.pallas_call(
         functools.partial(kernel, ndp, nslab, rows, width, pixel_scale),
         out_shape=(
-            jax.ShapeDtypeStruct((blk, C), F32),
-            jax.ShapeDtypeStruct((blk, C), F32),
-            jax.ShapeDtypeStruct((3, 9 * C), F32),
-            jax.ShapeDtypeStruct((1, C), F32),
-            jax.ShapeDtypeStruct((1, C), F32),
             jax.ShapeDtypeStruct((rows, width, C), BF16),
+            jax.ShapeDtypeStruct((2 * blk + 48, C), F32),
         ),
-        in_specs=[vmem, vmem, smem, smem, smem, smem, vmem, vmem, vmem, vmem, vmem],
-        out_specs=(vmem,) * 6,
+        in_specs=[anywhere, vmem, smem, smem, smem, smem, vmem, vmem, vmem, vmem, vmem],
+        out_specs=(anywhere, vmem),
         scratch_shapes=scratch,
         compiler_params=pltpu.CompilerParams(
             collective_id=0, has_side_effects=True, vmem_limit_bytes=60 * 2**20
@@ -541,6 +611,33 @@
         latents[0], image_grad[0], heights, widths, buckets, bucket_scale,
         conv_first, conv_second, conv_image, norm_gain[None], norm_bias[None],
     )
+    step_rows = 4
+    gw1, gw2, gci, gg, gb, gl = pl.pallas_call(
+        functools.partial(unload, blk, step_rows, width),
+        grid=(rows // step_rows,),
+        out_shape=(
+            jax.ShapeDtypeStruct((blk, C), F32),
+            jax.ShapeDtypeStruct((blk, C), F32),
+            jax.ShapeDtypeStruct((3, 9 * C), F32),
+            jax.ShapeDtypeStruct((1, C), F32),
+            jax.ShapeDtypeStruct((1, C), F32),
+            jax.ShapeDtypeStruct((rows, width, C), BF16),
+        ),
+        in_specs=[
+            pl.BlockSpec((step_rows, width, C), lambda i: (i, 0, 0)),
+            pl.BlockSpec((2 * blk + 48, C), lambda i: (0, 0)),
+        ],
+        out_specs=(
+            pl.BlockSpec((blk, C), lambda i: (0, 0)),
+            pl.BlockSpec((blk, C), lambda i: (0, 0)),
+            pl.BlockSpec((3, 9 * C), lambda i: (0, 0)),
+            pl.BlockSpec((1, C), lambda i: (0, 0)),
+            pl.BlockSpec((1, C), lambda i: (0, 0)),
+            pl.BlockSpec((step_rows, width, C), lambda i: (i, 0, 0)),
+        ),
+        scratch_shapes=[pltpu.VMEM((width, width), BF16)],
+        compiler_params=pltpu.CompilerParams(vmem_limit_bytes=16 * 2**20),
+    )(glp, pack)
     return gw1, gw2, gci, gg[0], gb[0], gl[None]
 
 

time: 85 us -> 75.7 us (0.89); the launches traced: 83.5 us -> 75.5 us
  local copies, waits for them, and re-layouts: 9.56 us -> 2.48 us
  Pallas kernels: 71.3 us -> 70.4 us
    unnamed x6 -> x4, local copies, waits for them, and re-layouts: 9.56 us -> 2.48 us
    pallas_call x1, Pallas kernels: 71.3 us -> 67.4 us  [shards(): pl.pallas_call(functools.partial(kernel, ndp, nslab, rows, width, pixel_s...]
    pallas_call x0 -> x1, Pallas kernels: none -> 3.03 us  [shards(): pl.pallas_call(functools.partial(unload, blk, step_rows, width), grid=(ro...]
where the time goes in v2:
time: 75.7 us; the launch traced here: 75.5 us
  Pallas kernels  70.4 us (93%)
  between operations  2.59 us (3%)
  local copies, waits for them, and re-layouts  2.48 us (3%)
    pallas_call x1, Pallas kernels, shards(): pl.pallas_call(functools.partial(kernel, ndp, nslab, rows, width, pixel_s...  67.4 us
    pallas_call x1, Pallas kernels, shards(): pl.pallas_call(functools.partial(unload, blk, step_rows, width), grid=(ro...  3.03 us
    unnamed x4, local copies, waits for them, and re-layouts  2.48 us

profile of v2, /device:TPU:0, one launch (start us, length us, event | category | flops | bytes accessed | tf_op | source)
XLA Modules:
  0.0 75.5 jit_solution(3412388904808630503)
XLA Ops:
  2.6 67.4 %shard_map.154 = (bf16[16,512,128]{2,1,0:T(8,128)(2,1)}, f32[192,128]{1,0:T(8,128)}) custom-call(bf16[16,512,128]{2,1,0:T(8,128)(2,1)} %bitcast.7, bf16[3,16,512]{2,1,0:T(8,128)(2,1)} %bitcast.9, s32[1]{0:T(128)S(6)} %copy.17.h_ref, s32[1]{0:T(128)S(6)} %copy.18.w_ref, s32[1]{0:T(128)S(6)} %copy.19.bk_ref, f32[8]{0:T(128)} %bs_ref.1, ...), custom_call_target="tpu_custom_call" | custom-call | flops 16000000000 | bytes 5242880 | tf_op jit(solution)/shard_map/pallas_call | solution.py:595
  70.0 0.0 copy-start
  70.0 1.6 %copy-done = bf16[16,512,128]{2,1,0:T(8,128)(2,1)S(1)} copy-done((bf16[16,512,128]{2,1,0:T(8,128)(2,1)S(1)}, bf16[16,512,128]{2,1,0:T(8,128)(2,1)}, u32[]{:S(2)}) %copy-start) | copy-done | bytes 2097176
  71.5 0.0 copy-start.1
  71.5 0.9 %copy-done.1 = f32[192,128]{1,0:T(8,128)S(1)} copy-done((f32[192,128]{1,0:T(8,128)S(1)}, f32[192,128]{1,0:T(8,128)}, u32[]{:S(2)}) %copy-start.1) | copy-done | bytes 98328
  72.4 3.0 %shard_map.155 = (f32[72,128]{1,0:T(8,128)}, f32[72,128]{1,0:T(8,128)}, f32[3,1152]{1,0:T(4,128)}, f32[1,128]{1,0:T(1,128)}, f32[1,128]{1,0:T(1,128)}, /*index=5*/bf16[16,512,128]{2,1,0:T(8,128)(2,1)}) custom-call(bf16[16,512,128]{2,1,0:T(8,128)(2,1)S(1)} %copy-done, f32[192,128]{1,0:T(8,128)S(1)} %copy-done.1), custom_call_target="tpu_custom_call" | custom-call | tf_op jit(solution)/shard_map/pallas_call | solution.py:615
Async XLA Ops:
  70.0 1.6 %copy-start = (bf16[16,512,128]{2,1,0:T(8,128)(2,1)S(1)}, bf16[16,512,128]{2,1,0:T(8,128)(2,1)}, u32[]{:S(2)}) copy-start(bf16[16,512,128]{2,1,0:T(8,128)(2,1)} %get-tuple-element.14.glp_ref) | copy-start | bytes 6291460
  71.5 0.9 %copy-start.1 = (f32[192,128]{1,0:T(8,128)S(1)}, f32[192,128]{1,0:T(8,128)}, u32[]{:S(2)}) copy-start(f32[192,128]{1,0:T(8,128)} %get-tuple-element.15.pack_ref) | copy-start | bytes 294916

commit v3 on v2

--- a/solution.py
+++ b/solution.py
@@ -34,9 +34,9 @@
 def kernel(
     ndp, nslab, rows, width, pixel_scale,
     lat_ref, img_ref, h_ref, w_ref, bk_ref, bs_ref, w1_ref, w2_ref, ci_ref, gain_ref, bias_ref,
-    out_ref, pack_ref,
-    lat, glp, perm, permt, col, latp, act, mid, actt, midt, h1, h2, gs, nact, b2, b1,
-    w4, ci4f, ci4, gstage, gimg, acc, flat, imgacc, sums, stat_send, stat_recv,
+    out_ref, gw_ref, gci_ref, gn_ref,
+    lat, lath, glp, slope0, slope1, perm, permt, col, latp, act, mid, actt, midt, h1, h2, gs, nact, b2, b1,
+    wi, wo, ci4f, ci4, gstage, gimg, acc, flat, imgacc, sums, stat_send, stat_recv,
     send_c, recv_c, send_a, recv_a, send_b, recv_b,
     small_c, small_rc, small_a, small_ra, small_b, small_rb,
     io_sem, halo_s, halo_r, stat_ss, stat_rs, c_ss, c_rs, a_ss, a_rs, b_ss, b_rs,
@@ -81,13 +81,21 @@
     count = (height * limit * PER_GROUP).astype(F32)
 
     def inside(r):
-        return col[...] < jnp.where(slab * rows + r < height, limit, 0)
-
-    def loop(lo, hi, body):
+        at = slab * rows + r
+        return col[...] < jnp.where((at >= 0) & (at < height), limit, 0)
+
+    def loop(lo, hi, body, unroll=1):
+        if hi - lo <= unroll:
+            for i in range(lo, hi):
+                body(i)
+            return
+        assert (hi - lo) % unroll == 0
+
         def step(i, _):
-            body(i)
+            for k in range(unroll):
+                body(lo + i * unroll + k)
             return 0
-        lax.fori_loop(lo, hi, step, 0)
+        lax.fori_loop(0, (hi - lo) // unroll, step, 0)
 
     def put(ref, row, a):
         ref[row, 1:t_count + 1] = a.reshape(t_count, S, C)
@@ -97,16 +105,20 @@
         high = pltpu.roll(a[:S].astype(F32), S - 1, 0)
         ref[row, t_count + 1] = jnp.where(sub == S - 1, 0.0, high).astype(BF16)
 
-    def halo(ref, e, d):
-        if d == 0:
-            src, dst, to = 1, last, lax.rem(slab + nslab - 1, nslab)
-        else:
-            src, dst, to = last - 1, 0, lax.rem(slab + 1, nslab)
+    def neighbour(src, dst, e, d):
+        to = lax.rem(slab + (1 if d else nslab - 1), nslab)
         return pltpu.make_async_remote_copy(
-            src_ref=ref.at[src], dst_ref=ref.at[dst],
-            send_sem=halo_s.at[e, d], recv_sem=halo_r.at[e, d],
+            src_ref=src, dst_ref=dst, send_sem=halo_s.at[e, d], recv_sem=halo_r.at[e, d],
             device_id={"slab": to}, device_id_type=MESH,
         )
+
+    def halo(ref, e, d):
+        src, dst = (last - 1, 0) if d else (1, last)
+        return neighbour(ref.at[src], ref.at[dst], e, d)
+
+    def latent_halo(d):
+        src = lat_ref.at[pl.ds(rows - 2 if d else 0, 2)]
+        return neighbour(src, lath.at[1 - d], 0, d)
 
     def halo_start(ref, e):
         for d in range(2):
@@ -165,23 +177,29 @@
     col[...] = (j_i % S) * t_count + j_i // S
 
     def ends(body):
-        loop(0, 2, lambda k: body(k * (npair - 1)))
+        body(0)
+        body(npair - 1)
+
+    def input_rows(r0, pair):
+        x = dot(perm[...], jnp.concatenate(pair, axis=1))
+        kept = []
+        for k in range(2):
+            v = x[:, k * C:(k + 1) * C]
+            a = jnp.where(inside(r0 + k), v * sigmoid(v), 0.0).astype(BF16)
+            put(act, r0 + k + 2, a)
+            kept.append(v.astype(BF16))
+        return kept
 
     def stage_input(i):
         latents_in(i).wait()
-        x = dot(perm[...], jnp.concatenate([lat[2 * i], lat[2 * i + 1]], axis=1))
-        for k in range(2):
-            r = 2 * i + k
-            v = x[:, k * C:(k + 1) * C]
-            latp[r] = v.astype(BF16)
-            a = jnp.where(inside(r), v * sigmoid(v), 0.0).astype(BF16)
-            put(act, r + 1, a)
-            actt[r + 1] = a.T
-
-    ends(stage_input)
+        kept = input_rows(2 * i, [lat[2 * i], lat[2 * i + 1]])
+        for k in range(2):
+            latp[2 * i + k] = kept[k]
+
     pl.semaphore_wait(barrier, ndp + nslab - 2)
-    halo_start(act, 0)
-    loop(1, npair - 1, stage_input)
+    for d in range(2):
+        latent_halo(d).start()
+    loop(0, npair, stage_input, 4)
 
     scale = bs_ref[bk_ref[0]]
     row3 = lax.broadcasted_iota(jnp.int32, (3, rows, width), 1) + slab * rows
@@ -204,20 +222,26 @@
 
     halo_start(gimg, 1)
 
-    for c, (ref, flip) in enumerate(((w1_ref, False), (w2_ref, False), (w2_ref, True), (w1_ref, True))):
-        for j in range(4):
+    zero = jnp.zeros((C, C), BF16)
+
+    def weights(c, ref, flip):
+        def tap(p, q):
+            n = 3 * p + q
+            return ref[(8 - n) * C:(9 - n) * C, :].T if flip else ref[n * C:(n + 1) * C, :]
+
+        for j in range(1, 3):
             for q in range(3):
-                at = (j * 3 + q) * C
+                at = (3 * (j - 1) + q) * C
                 for k in range(2):
-                    if 0 <= j - k <= 2:
-                        tap = 3 * (j - k) + q
-                        if flip:
-                            b = ref[(8 - tap) * C:(9 - tap) * C, :].T
-                        else:
-                            b = ref[tap * C:(tap + 1) * C, :]
-                    else:
-                        b = jnp.zeros((C, C), BF16)
-                    w4[c, at:at + C, k * C:(k + 1) * C] = b
+                    wi[c, at:at + C, k * C:(k + 1) * C] = tap(j - k, q)
+        for k in range(2):
+            wo[c, k, 0:C, 0:C] = tap(2 * k, 0)
+            wo[c, k, 0:C, C:] = zero
+            wo[c, k, C:, 0:C] = tap(2 * k, 1)
+            wo[c, k, C:, C:] = tap(2 * k, 2)
+
+    weights(0, w1_ref, False)
+    weights(1, w2_ref, False)
     ci4f[...] = jnp.zeros_like(ci4f)
     for p in range(3):
         for q in range(3):
@@ -229,28 +253,28 @@
 
     def conv(src, c, i):
         taps = [
-            src[2 * i + j, q:q + t_count].reshape(width, C) for j in range(4) for q in range(3)
+            src[2 * i + j, q:q + t_count].reshape(width, C) for j in (1, 2) for q in range(3)
         ]
-        return dot(jnp.concatenate(taps, axis=1), w4[c])
+        inner = dot(jnp.concatenate(taps, axis=1), wi[c])
+        done = []
+        for k in range(2):
+            pair = [
+                src[2 * i + 3 * k, q:q + t_count + 1].reshape(width + S, C) for q in range(2)
+            ]
+            outer = dot(jnp.concatenate(pair, axis=1), wo[c, k])
+            done.append(inner[:, k * C:(k + 1) * C] + outer[0:width, 0:C] + outer[S:, C:])
+        return done
 
     def stage_one(i):
         y = conv(act, 0, i)
         for k in range(2):
-            r = 2 * i + k
-            hb = y[:, k * C:(k + 1) * C].astype(BF16)
-            h1[r] = hb
+            hb = y[k].astype(BF16)
+            h1[2 * i + k] = hb
             hf = hb.astype(F32)
-            m = jnp.where(inside(r), hf * sigmoid(hf), 0.0).astype(BF16)
-            put(mid, r + 1, m)
-            midt[r + 1] = m.T
-
-    loop(1, npair // 2, stage_one)
-    halo_wait(act, 0)
-    ends(stage_one)
-    halo_start(mid, 2)
-    loop(npair // 2, npair - 1, stage_one)
-    for e in (0, last):
-        actt[e] = act[e, 1:t_count + 1].reshape(width, C).T
+            m = jnp.where(inside(2 * i - 1 + k), hf * sigmoid(hf), 0.0).astype(BF16)
+            put(mid, 2 * i + k, m)
+
+    loop(1, npair, stage_one, npair - 1)
 
     sums[...] = jnp.zeros_like(sums)
 
@@ -261,14 +285,20 @@
         y = conv(mid, 1, i)
         for k in range(2):
             r = 2 * i + k
-            v = y[:, k * C:(k + 1) * C] + latp[r].astype(F32)
+            v = y[k] + latp[r].astype(F32)
             h2[r] = v
             masked = jnp.where(inside(r), v, 0.0)
             sums[0] += fold(masked)
             sums[1] += fold(masked * v)
 
-    loop(1, npair - 1, stage_two)
-    halo_wait(mid, 2)
+    loop(1, npair - 1, stage_two, 3)
+
+    for d in range(2):
+        latent_halo(d).wait()
+    input_rows(-2, [lath[0, 0], lath[0, 1]])
+    input_rows(rows, [lath[1, 0], lath[1, 1]])
+    stage_one(0)
+    stage_one(npair)
     ends(stage_two)
 
     def stats(e):
@@ -298,11 +328,20 @@
             preferred_element_type=F32,
         )
         for k in range(2):
-            gs[2 * i + k] = y[:, k * C:(k + 1) * C]
-
-    loop(0, npair, stage_image)
-    for e in (0, last):
-        midt[e] = mid[e, 1:t_count + 1].reshape(width, C).T
+            gs[2 * i + k] = jnp.where(inside(2 * i + k), y[:, k * C:(k + 1) * C], 0.0)
+
+    loop(0, npair, stage_image, 4)
+    weights(2, w2_ref, True)
+    weights(3, w1_ref, True)
+
+    def stage_slopes(r):
+        here = inside(r)
+        for kept, out in ((h1[r + 1], slope1), (latp[r], slope0)):
+            v = kept.astype(F32)
+            t = sigmoid(v)
+            out[r] = jnp.where(here, t + v * t * (1.0 - t), 0.0)
+
+    loop(0, rows, stage_slopes)
     wait()
 
     total = stat_total(0)
@@ -311,18 +350,18 @@
     gain = gain_ref[...]
     bias = bias_ref[...]
 
+    c1 = rstd * gain
+
     def stage_norm(r):
-        n = (h2[r] - mean) * rstd
-        v = n * gain + bias
+        centred = h2[r] - mean
+        v = centred * c1 + bias
         s = sigmoid(v)
         vs = v * s
-        here = inside(r)
-        nact[r] = jnp.where(here, vs, 0.0).astype(BF16)
-        g = jnp.where(here, gs[r] * (s + vs * (1.0 - s)), 0.0)
-        h2[r] = n
+        nact[r] = jnp.where(inside(r), vs, 0.0).astype(BF16)
+        g = gs[r] * (s + vs * (1.0 - s))
         gs[r] = g
         sums[2] += fold(g)
-        sums[3] += fold(g * n)
+        sums[3] += fold(g * centred)
 
     loop(0, rows, stage_norm)
     start, wait = stats(1)
@@ -336,26 +375,34 @@
             jnp.concatenate([nact[2 * i], nact[2 * i + 1]], axis=1),
         )
 
-    loop(0, npair, stage_imgw)
+    loop(0, npair, stage_imgw, 4)
     flat[0:48] = imgacc[0:48, 0:C] + imgacc[16:64, C:2 * C]
-    flat[9:10] = jnp.sum(sums[3], axis=0, keepdims=True)
+    flat[9:10] = jnp.sum(sums[3], axis=0, keepdims=True) * rstd
     flat[10:11] = jnp.sum(sums[2], axis=0, keepdims=True)
     small_c[...] = flat[0:48].astype(BF16)
     to_core(small_c, small_rc, 0).start()
+
+    def transposed(src, off, dst):
+        def body(row):
+            dst[row] = src[row + off, 1:t_count + 1].reshape(width, C).T
+        loop(0, last + 1, body, 3)
+
+    transposed(mid, 0, midt)
+    transposed(act, 1, actt)
     wait()
 
     total = stat_total(1)
-    c1 = rstd * gain
     c0 = rstd * (group_total(total[0:1] * gain) / count)
-    c2 = rstd * (group_total(total[1:2] * gain) / count)
+    c2 = rstd * rstd * (rstd * group_total(total[1:2] * gain) / count)
 
     def stage_grad_two(r):
-        g = jnp.where(inside(r), gs[r] * c1 - c0 - h2[r] * c2, 0.0).astype(BF16)
+        g = jnp.where(inside(r), gs[r] * c1 - c0 - (h2[r] - mean) * c2, 0.0).astype(BF16)
         put(b2, r + 1, g)
 
-    loop(0, 2, lambda k: stage_grad_two(k * (rows - 1)))
+    stage_grad_two(0)
+    stage_grad_two(rows - 1)
     halo_start(b2, 3)
-    loop(1, rows - 1, stage_grad_two)
+    loop(1, rows - 1, stage_grad_two, 2)
 
     def weight_grad(at, b):
         acc[...] = jnp.zeros_like(acc)
@@ -363,23 +410,32 @@
         def piece(row, q):
             return b[row, 2 - q:2 - q + t_count].reshape(width, C)
 
+        many = min(4, npair)
+
         def body(i):
+            firsts = [2 * (i * many + u) for u in range(many)]
             lhs = jnp.concatenate(
-                [at[pl.ds(2 * i + k, 3)].reshape(3 * C, width) for k in range(2)], axis=1
+                [at[pl.ds(r + k, 3)].reshape(3 * C, width) for r in firsts for k in range(2)], axis=1
             )
             rhs = jnp.concatenate(
                 [
-                    jnp.concatenate([piece(2 * i + 1 + k, q) for q in range(2)], axis=1)
-                    for k in range(2)
+                    jnp.concatenate([piece(r + 1 + k, q) for q in range(2)], axis=1)
+                    for r in firsts for k in range(2)
                 ],
                 axis=0,
             )
             acc[:, 0:2 * C] += dot(lhs, rhs)
-            rhs = jnp.concatenate([piece(2 * i + 1 + k, 2) for k in range(2)], axis=1)
-            z = dot(at[pl.ds(2 * i, 4)].reshape(4 * C, width), rhs)
+            lhs = jnp.concatenate(
+                [at[pl.ds(r, 4)].reshape(4 * C, width) for r in firsts], axis=1
+            )
+            rhs = jnp.concatenate(
+                [jnp.concatenate([piece(r + 1 + k, 2) for k in range(2)], axis=1) for r in firsts],
+                axis=0,
+            )
+            z = dot(lhs, rhs)
             acc[:, 2 * C:] += z[0:3 * C, 0:C] + z[C:, C:]
 
-        loop(0, npair, body)
+        loop(0, npair // many, body)
 
     def scatter(e):
         for p in range(3):
@@ -421,7 +477,7 @@
         part = recv_b[e, 0].astype(F32)
         for k in range(1, nslab):
             part = part + recv_b[e, k].astype(F32)
-        pack_ref[e * blk:(e + 1) * blk] = part[0:blk] * pixel_scale
+        gw_ref[1 - e] = part[0:blk] * pixel_scale
 
     send_c[...] = jnp.zeros_like(send_c)
     weight_grad(midt, b2)
@@ -433,24 +489,38 @@
     small_start, small_wait = to_chips(lambda peer: small_a, small_ra, 0)
     small_start()
 
-    halo_wait(b2, 3)
-
     def stage_grad_one(i):
         y = conv(b2, 2, i)
         for k in range(2):
             r = 2 * i + k
-            v = h1[r].astype(F32)
-            s = sigmoid(v)
-            slope = s + v * s * (1.0 - s)
-            g = jnp.where(inside(r), y[:, k * C:(k + 1) * C] * slope, 0.0).astype(BF16)
-            put(b1, r + 1, g)
-
+            put(b1, r + 1, (y[k] * slope1[r]).astype(BF16))
+
+    loop(1, npair - 1, stage_grad_one, 3)
+    halo_wait(b2, 3)
     ends(stage_grad_one)
     halo_start(b1, 4)
     second.wait()
     second_wait = chips(0)
-    loop(1, npair - 1, stage_grad_one)
-
+
+    weight_grad(actt, b1)
+    first = scatter(1)
+
+    def stage_latents(i):
+        y = conv(b1, 3, i)
+        done = []
+        for k in range(2):
+            r = 2 * i + k
+            g = y[k] * slope0[r]
+            own = b2[r + 1, 1:t_count + 1].reshape(width, C).astype(F32)
+            done.append((own + g).astype(BF16))
+        z = dot(permt[...], jnp.concatenate(done, axis=1)).astype(BF16)
+        for k in range(2):
+            glp[2 * i + k] = z[:, k * C:(k + 1) * C]
+        latents_out(i).start()
+
+    loop(1, 1 + (npair - 2) // 2, stage_latents, 3)
+    first.wait()
+    first_wait = chips(1)
     small_wait()
     part = small_ra[0].astype(F32)
     for k in range(1, nchip):
@@ -464,35 +534,23 @@
     second_wait()
     second_b_wait = gather(0)
 
-    weight_grad(actt, b1)
-    first = scatter(1)
+    loop(1 + (npair - 2) // 2, npair - 1, stage_latents, 3)
     halo_wait(b1, 4)
-
-    def stage_latents(i):
-        y = conv(b1, 3, i)
-        for k in range(2):
-            r = 2 * i + k
-            v = latp[r].astype(F32)
-            s = sigmoid(v)
-            slope = s + v * s * (1.0 - s)
-            g = jnp.where(inside(r), y[:, k * C:(k + 1) * C] * slope, 0.0)
-            own = b2[r + 1, 1:t_count + 1].reshape(width, C).astype(F32)
-            glp[r] = (own + g).astype(BF16)
-        latents_out(i).start()
-
-    loop(0, npair // 4, stage_latents)
-    first.wait()
-    first_wait = chips(1)
-    loop(npair // 4, npair * 5 // 8, stage_latents)
+    ends(stage_latents)
     first_wait()
     first_b_wait = gather(1)
-    loop(npair * 5 // 8, npair, stage_latents)
 
     small_b_wait()
     part = small_rb[0].astype(F32)
     for k in range(1, nslab):
         part = part + small_rb[k].astype(F32)
-    pack_ref[2 * blk:2 * blk + 48] = part * pixel_scale
+    part = part * pixel_scale
+    gn_ref[0] = part[9:10]
+    gn_ref[1] = part[10:11]
+    for p in range(3):
+        for q in range(3):
+            at = (2 - p) * 16 + q * 3
+            gci_ref[:, (3 * p + q) * C:(3 * p + q + 1) * C] = part[at:at + 3]
     second_b_wait()
     finish(0)
     first_b_wait()
@@ -500,28 +558,23 @@
     loop(0, npair, lambda i: latents_out(i).wait())
 
 
-def unload(blk, step_rows, width, glp_ref, pack_ref, gw1_ref, gw2_ref, gci_ref, gg_ref, gb_ref, gl_ref, permt):
-    t_count = width // S
-
-    @pl.when(pl.program_id(0) == 0)
-    def _():
-        a_i = lax.broadcasted_iota(jnp.int32, (width, width), 0)
-        b_i = lax.broadcasted_iota(jnp.int32, (width, width), 1)
-        permt[...] = jnp.where((b_i % S) * t_count + b_i // S == a_i, 1.0, 0.0).astype(BF16)
-        gw1_ref[...] = pack_ref[blk:2 * blk]
-        gw2_ref[...] = pack_ref[0:blk]
-        base = 2 * blk
-        gg_ref[...] = pack_ref[base + 9:base + 10]
-        gb_ref[...] = pack_ref[base + 10:base + 11]
-        for p in range(3):
-            for q in range(3):
-                at = base + (2 - p) * 16 + q * 3
-                gci_ref[:, (3 * p + q) * C:(3 * p + q + 1) * C] = pack_ref[at:at + 3]
-
-    for i in range(step_rows // 2):
-        z = dot(permt[...], jnp.concatenate([glp_ref[2 * i], glp_ref[2 * i + 1]], axis=1))
-        for k in range(2):
-            gl_ref[2 * i + k] = z[:, k * C:(k + 1) * C].astype(BF16)
+def unload(parts, gl_in, gw_in, gci_in, gn_in, gw1, gw2, gci, gg, gb, gl, gl_buf, gw_buf, gci_buf, gn_buf, sem):
+    step = gl_buf.shape[0] // parts
+    moves = [(gw_in.at[0], gw_buf.at[0], gw1), (gw_in.at[1], gw_buf.at[1], gw2), (gci_in, gci_buf, gci)]
+    moves += [(gn_in.at[0], gn_buf.at[0], gg), (gn_in.at[1], gn_buf.at[1], gb)]
+    for i in range(parts):
+        rows = pl.ds(i * step, step)
+        moves.append((gl_in.at[rows], gl_buf.at[rows], gl.at[rows]))
+    into = [pltpu.make_async_copy(m[0], m[1], sem.at[0, i]) for i, m in enumerate(moves)]
+    back = [pltpu.make_async_copy(m[1], m[2], sem.at[1, i]) for i, m in enumerate(moves)]
+    order = list(range(5, 5 + parts)) + list(range(5))
+    for i in order:
+        into[i].start()
+    for i in order:
+        into[i].wait()
+        back[i].start()
+    for i in order:
+        back[i].wait()
 
 
 def shards(
@@ -539,24 +592,29 @@
     smem = pl.BlockSpec(memory_space=pltpu.SMEM)
     nchip = ndp // 2
     edge = (rows + 2, t_count + 2, S, C)
+    wide = (rows + 4, t_count + 2, S, C)
     scratch = [
         pltpu.VMEM((rows, width, C), BF16),
+        pltpu.VMEM((2, 2, width, C), BF16),
         pltpu.VMEM((rows, width, C), BF16),
+        pltpu.VMEM((rows, width, C), F32),
+        pltpu.VMEM((rows, width, C), F32),
         pltpu.VMEM((width, width), BF16),
         pltpu.VMEM((width, width), BF16),
         pltpu.VMEM((width, C), jnp.int32),
         pltpu.VMEM((rows, width, C), BF16),
-        pltpu.VMEM(edge, BF16),
+        pltpu.VMEM(wide, BF16),
         pltpu.VMEM(edge, BF16),
         pltpu.VMEM((rows + 2, C, width), BF16),
         pltpu.VMEM((rows + 2, C, width), BF16),
-        pltpu.VMEM((rows, width, C), BF16),
+        pltpu.VMEM((rows + 2, width, C), BF16),
         pltpu.VMEM((rows, width, C), F32),
         pltpu.VMEM((rows, width, C), F32),
         pltpu.VMEM((rows, width, C), BF16),
         pltpu.VMEM(edge, BF16),
         pltpu.VMEM(edge, BF16),
-        pltpu.VMEM((4, 12 * C, 2 * C), BF16),
+        pltpu.VMEM((4, 6 * C, 2 * C), BF16),
+        pltpu.VMEM((4, 2, 2 * C, 2 * C), BF16),
         pltpu.VMEM((64, 2 * C), F32),
         pltpu.VMEM((64, 2 * C), BF16),
         pltpu.VMEM((width // C, 16 * rows, C), F32),
@@ -592,14 +650,16 @@
         pltpu.SemaphoreType.DMA((3, nslab)),
     ]
     anywhere = pl.BlockSpec(memory_space=pl.ANY)
-    glp, pack = pl.pallas_call(
+    staged = pl.pallas_call(
         functools.partial(kernel, ndp, nslab, rows, width, pixel_scale),
         out_shape=(
             jax.ShapeDtypeStruct((rows, width, C), BF16),
-            jax.ShapeDtypeStruct((2 * blk + 48, C), F32),
+            jax.ShapeDtypeStruct((2, blk, C), F32),
+            jax.ShapeDtypeStruct((3, 9 * C), F32),
+            jax.ShapeDtypeStruct((2, 1, C), F32),
         ),
         in_specs=[anywhere, vmem, smem, smem, smem, smem, vmem, vmem, vmem, vmem, vmem],
-        out_specs=(anywhere, vmem),
+        out_specs=(anywhere, vmem, vmem, vmem),
         scratch_shapes=scratch,
         compiler_params=pltpu.CompilerParams(
             collective_id=0, has_side_effects=True, vmem_limit_bytes=60 * 2**20
@@ -611,10 +671,9 @@
         latents[0], image_grad[0], heights, widths, buckets, bucket_scale,
         conv_first, conv_second, conv_image, norm_gain[None], norm_bias[None],
     )
-    step_rows = 4
+    parts = 4
     gw1, gw2, gci, gg, gb, gl = pl.pallas_call(
-        functools.partial(unload, blk, step_rows, width),
-        grid=(rows // step_rows,),
+        functools.partial(unload, parts),
         out_shape=(
             jax.ShapeDtypeStruct((blk, C), F32),
             jax.ShapeDtypeStruct((blk, C), F32),
@@ -623,21 +682,17 @@
             jax.ShapeDtypeStruct((1, C), F32),
             jax.ShapeDtypeStruct((rows, width, C), BF16),
         ),
-        in_specs=[
-            pl.BlockSpec((step_rows, width, C), lambda i: (i, 0, 0)),
-            pl.BlockSpec((2 * blk + 48, C), lambda i: (0, 0)),
+        in_specs=[anywhere] * 4,
+        out_specs=(anywhere,) * 6,
+        scratch_shapes=[
+            pltpu.VMEM((rows, width, C), BF16),
+            pltpu.VMEM((2, blk, C), F32),
+            pltpu.VMEM((3, 9 * C), F32),
+            pltpu.VMEM((2, 1, C), F32),
+            pltpu.SemaphoreType.DMA((2, parts + 5)),
         ],
-        out_specs=(
-            pl.BlockSpec((blk, C), lambda i: (0, 0)),
-            pl.BlockSpec((blk, C), lambda i: (0, 0)),
-            pl.BlockSpec((3, 9 * C), lambda i: (0, 0)),
-            pl.BlockSpec((1, C), lambda i: (0, 0)),
-            pl.BlockSpec((1, C), lambda i: (0, 0)),
-            pl.BlockSpec((step_rows, width, C), lambda i: (i, 0, 0)),
-        ),
-        scratch_shapes=[pltpu.VMEM((width, width), BF16)],
-        compiler_params=pltpu.CompilerParams(vmem_limit_bytes=16 * 2**20),
-    )(glp, pack)
+        compiler_params=pltpu.CompilerParams(vmem_limit_bytes=60 * 2**20),
+    )(*staged)
     return gw1, gw2, gci, gg[0], gb[0], gl[None]
 
 

time: 75.7 us -> 64.4 us (0.85)
  Pallas kernels: 70.4 us -> 61.4 us
  local copies, waits for them, and re-layouts: 2.48 us -> 0 us
    pallas_call x1, Pallas kernels: 67.4 us -> 58.9 us  [shards(): pl.pallas_call(functools.partial(kernel, ndp, nslab, rows, width, pixel_s...]
    unnamed x4 -> x0, local copies, waits for them, and re-layouts: 2.48 us -> none
where the time goes in v3:
time: 64.4 us; the launch traced here: 64.2 us
  Pallas kernels  61.4 us (95%)
  between operations  2.74 us (4%)
    pallas_call x1, Pallas kernels, shards(): pl.pallas_call(functools.partial(kernel, ndp, nslab, rows, width, pixel_s...  58.9 us
    pallas_call x1, Pallas kernels, shards(): pl.pallas_call(functools.partial(unload, parts), out_shape=(jax.ShapeDtyp...  2.53 us

profile of v3, /device:TPU:0, one launch (start us, length us, event | category | flops | bytes accessed | tf_op | source)
XLA Modules:
  0.0 64.2 jit_solution(6918492175002547178)
XLA Ops:
  2.6 58.9 %shard_map.154 = (bf16[16,512,128]{2,1,0:T(8,128)(2,1)}, f32[2,72,128]{2,1,0:T(8,128)}, f32[3,1152]{1,0:T(4,128)}, f32[2,1,128]{2,1,0:T(1,128)}) custom-call(bf16[16,512,128]{2,1,0:T(8,128)(2,1)} %bitcast.7, bf16[3,16,512]{2,1,0:T(8,128)(2,1)} %bitcast.9, s32[1]{0:T(128)S(6)} %copy.17.h_ref, s32[1]{0:T(128)S(6)} %copy.18.w_ref, s32[1]{0:T(128)S(6)} %copy.19.bk_ref, ...), custom_call_target="tpu_custom_call" | custom-call | flops 16000000000 | bytes 5242880 | tf_op jit(solution)/shard_map/pallas_call | solution.py:653
  61.5 2.5 %shard_map.155 = (f32[72,128]{1,0:T(8,128)}, f32[72,128]{1,0:T(8,128)}, f32[3,1152]{1,0:T(4,128)}, f32[1,128]{1,0:T(1,128)}, f32[1,128]{1,0:T(1,128)}, /*index=5*/bf16[16,512,128]{2,1,0:T(8,128)(2,1)}) custom-call(bf16[16,512,128]{2,1,0:T(8,128)(2,1)} %get-tuple-element.16.gl_in, f32[2,72,128]{2,1,0:T(8,128)} %get-tuple-element.17.gw_in, ...), custom_call_target="tpu_custom_call" | custom-call | tf_op jit(solution)/shard_map/pallas_call | solution.py:675

commit v4 on v3

--- a/solution.py
+++ b/solution.py
@@ -33,9 +33,9 @@
 
 def kernel(
     ndp, nslab, rows, width, pixel_scale,
-    lat_ref, img_ref, h_ref, w_ref, bk_ref, bs_ref, w1_ref, w2_ref, ci_ref, gain_ref, bias_ref,
+    lat_ref, img_in, h_ref, w_ref, bk_ref, bs_ref, w1_in, w2_in, ci_ref, gain_ref, bias_ref,
     out_ref, gw_ref, gci_ref, gn_ref,
-    lat, lath, glp, slope0, slope1, perm, permt, col, latp, act, mid, actt, midt, h1, h2, gs, nact, b2, b1,
+    img_ref, w1_ref, w2_ref, load_sem, lat, lath, glp, slope0, slope1, perm, permt, col, latp, act, mid, actt, midt, h1, h2, gs, nact, b2, b1,
     wi, wo, ci4f, ci4, gstage, gimg, acc, flat, imgacc, sums, stat_send, stat_recv,
     send_c, recv_c, send_a, recv_a, send_b, recv_b,
     small_c, small_rc, small_a, small_ra, small_b, small_rb,
@@ -59,9 +59,13 @@
         part = pl.ds(2 * i, 2)
         return pltpu.make_async_copy(glp.at[part], out_ref.at[part], io_sem.at[1, i])
 
-    latents_in(0).start()
-    latents_in(npair - 1).start()
-    lax.fori_loop(1, npair - 1, lambda i, _: (latents_in(i).start(), 0)[1], 0)
+    lax.fori_loop(0, npair, lambda i, _: (latents_in(i).start(), 0)[1], 0)
+    loads = [
+        pltpu.make_async_copy(src, dst, load_sem.at[i])
+        for i, (src, dst) in enumerate(((img_in, img_ref), (w1_in, w1_ref), (w2_in, w2_ref)))
+    ]
+    for copy in loads:
+        copy.start()
 
     barrier = pltpu.get_barrier_semaphore()
 
@@ -120,13 +124,33 @@
         src = lat_ref.at[pl.ds(rows - 2 if d else 0, 2)]
         return neighbour(src, lath.at[1 - d], 0, d)
 
+    above, below = slab > 0, slab < nslab - 1
+
+    def exchange_start(copy):
+        @pl.when(above)
+        def _():
+            copy(0).start()
+
+        @pl.when(below)
+        def _():
+            copy(1).start()
+
+    def exchange_wait(copy):
+        @pl.when(above)
+        def _():
+            copy(0).wait_send()
+            copy(1).wait_recv()
+
+        @pl.when(below)
+        def _():
+            copy(1).wait_send()
+            copy(0).wait_recv()
+
     def halo_start(ref, e):
-        for d in range(2):
-            halo(ref, e, d).start()
+        exchange_start(lambda d: halo(ref, e, d))
 
     def halo_wait(ref, e):
-        for d in range(2):
-            halo(ref, e, d).wait()
+        exchange_wait(lambda d: halo(ref, e, d))
 
         @pl.when(slab == 0)
         def _():
@@ -191,16 +215,24 @@
         return kept
 
     def stage_input(i):
-        latents_in(i).wait()
         kept = input_rows(2 * i, [lat[2 * i], lat[2 * i + 1]])
         for k in range(2):
             latp[2 * i + k] = kept[k]
 
+    many = npair // 2
+
+    def stage_inputs(g):
+        for k in range(many):
+            latents_in(many * g + k).wait()
+        for k in range(many):
+            stage_input(many * g + k)
+
+    loop(0, 2, stage_inputs)
     pl.semaphore_wait(barrier, ndp + nslab - 2)
-    for d in range(2):
-        latent_halo(d).start()
-    loop(0, npair, stage_input, 4)
-
+    exchange_start(latent_halo)
+
+    for copy in loads:
+        copy.wait()
     scale = bs_ref[bk_ref[0]]
     row3 = lax.broadcasted_iota(jnp.int32, (3, rows, width), 1) + slab * rows
     lane3 = lax.broadcasted_iota(jnp.int32, (3, rows, width), 2)
@@ -293,8 +325,16 @@
 
     loop(1, npair - 1, stage_two, 3)
 
-    for d in range(2):
-        latent_halo(d).wait()
+    exchange_wait(latent_halo)
+
+    @pl.when(slab == 0)
+    def _():
+        lath[0] = jnp.zeros(lath.shape[1:], lath.dtype)
+
+    @pl.when(slab == nslab - 1)
+    def _():
+        lath[1] = jnp.zeros(lath.shape[1:], lath.dtype)
+
     input_rows(-2, [lath[0, 0], lath[0, 1]])
     input_rows(rows, [lath[1, 0], lath[1, 1]])
     stage_one(0)
@@ -334,14 +374,14 @@
     weights(2, w2_ref, True)
     weights(3, w1_ref, True)
 
-    def stage_slopes(r):
-        here = inside(r)
-        for kept, out in ((h1[r + 1], slope1), (latp[r], slope0)):
-            v = kept.astype(F32)
+    def slopes(kept, off, out):
+        def body(r):
+            v = kept[r + off].astype(F32)
             t = sigmoid(v)
-            out[r] = jnp.where(here, t + v * t * (1.0 - t), 0.0)
-
-    loop(0, rows, stage_slopes)
+            out[r] = jnp.where(inside(r), t + v * t * (1.0 - t), 0.0)
+        loop(0, rows, body)
+
+    slopes(h1, 1, slope1)
     wait()
 
     total = stat_total(0)
@@ -387,6 +427,7 @@
             dst[row] = src[row + off, 1:t_count + 1].reshape(width, C).T
         loop(0, last + 1, body, 3)
 
+    slopes(latp, 0, slope0)
     transposed(mid, 0, midt)
     transposed(act, 1, actt)
     wait()
@@ -483,24 +524,25 @@
     weight_grad(midt, b2)
     second = scatter(0)
 
+    def stage_grad_one(i):
+        y = conv(b2, 2, i)
+        for k in range(2):
+            r = 2 * i + k
+            put(b1, r + 1, (y[k] * slope1[r]).astype(BF16))
+
+    middle = 1 + (npair - 2) // 2
+    loop(1, middle, stage_grad_one, 3)
+    second.wait()
+    second_wait = chips(0)
     to_core(small_c, small_rc, 0).wait()
     small_a[...] = (small_c[...].astype(F32) + small_rc[...].astype(F32)).astype(BF16)
     small_ra[chip] = small_a[...]
     small_start, small_wait = to_chips(lambda peer: small_a, small_ra, 0)
     small_start()
-
-    def stage_grad_one(i):
-        y = conv(b2, 2, i)
-        for k in range(2):
-            r = 2 * i + k
-            put(b1, r + 1, (y[k] * slope1[r]).astype(BF16))
-
-    loop(1, npair - 1, stage_grad_one, 3)
+    loop(middle, npair - 1, stage_grad_one, 3)
     halo_wait(b2, 3)
     ends(stage_grad_one)
     halo_start(b1, 4)
-    second.wait()
-    second_wait = chips(0)
 
     weight_grad(actt, b1)
     first = scatter(1)
@@ -516,9 +558,13 @@
         z = dot(permt[...], jnp.concatenate(done, axis=1)).astype(BF16)
         for k in range(2):
             glp[2 * i + k] = z[:, k * C:(k + 1) * C]
-        latents_out(i).start()
-
-    loop(1, 1 + (npair - 2) // 2, stage_latents, 3)
+
+    def latents_group(lo, hi):
+        loop(lo, hi, stage_latents, hi - lo)
+        for i in range(lo, hi):
+            latents_out(i).start()
+
+    latents_group(1, 2)
     first.wait()
     first_wait = chips(1)
     small_wait()
@@ -533,12 +579,12 @@
     small_b_start()
     second_wait()
     second_b_wait = gather(0)
-
-    loop(1 + (npair - 2) // 2, npair - 1, stage_latents, 3)
+    latents_group(2, npair - 1)
+    first_wait()
+    first_b_wait = gather(1)
     halo_wait(b1, 4)
     ends(stage_latents)
-    first_wait()
-    first_b_wait = gather(1)
+    ends(lambda i: latents_out(i).start())
 
     small_b_wait()
     part = small_rb[0].astype(F32)
@@ -594,6 +640,10 @@
     edge = (rows + 2, t_count + 2, S, C)
     wide = (rows + 4, t_count + 2, S, C)
     scratch = [
+        pltpu.VMEM(image_grad.shape[1:], BF16),
+        pltpu.VMEM(conv_first.shape, BF16),
+        pltpu.VMEM(conv_second.shape, BF16),
+        pltpu.SemaphoreType.DMA((3,)),
         pltpu.VMEM((rows, width, C), BF16),
         pltpu.VMEM((2, 2, width, C), BF16),
         pltpu.VMEM((rows, width, C), BF16),
@@ -658,7 +708,7 @@
             jax.ShapeDtypeStruct((3, 9 * C), F32),
             jax.ShapeDtypeStruct((2, 1, C), F32),
         ),
-        in_specs=[anywhere, vmem, smem, smem, smem, smem, vmem, vmem, vmem, vmem, vmem],
+        in_specs=[anywhere, anywhere, smem, smem, smem, smem, anywhere, anywhere, vmem, vmem, vmem],
         out_specs=(anywhere, vmem, vmem, vmem),
         scratch_shapes=scratch,
         compiler_params=pltpu.CompilerParams(

time: 64.4 us -> 62.7 us (0.974)
  Pallas kernels: 61.4 us -> 59.7 us
    pallas_call x1, Pallas kernels: 58.9 us -> 57.2 us  [shards(): pl.pallas_call(functools.partial(kernel, ndp, nslab, rows, width, pixel_s...]
where the time goes in v4:
time: 62.7 us; the launch traced here: 62.4 us
  Pallas kernels  59.7 us (95%)
  between operations  2.74 us (4%)
    pallas_call x1, Pallas kernels, shards(): pl.pallas_call(functools.partial(kernel, ndp, nslab, rows, width, pixel_s...  57.2 us
    pallas_call x1, Pallas kernels, shards(): pl.pallas_call(functools.partial(unload, parts), out_shape=(jax.ShapeDtyp...  2.53 us

profile of v4, /device:TPU:0, one launch (start us, length us, event | category | flops | bytes accessed | tf_op | source)
XLA Modules:
  0.0 62.4 jit_solution(8597670772044183043)
XLA Ops:
  2.6 57.2 %shard_map.154 = (bf16[16,512,128]{2,1,0:T(8,128)(2,1)}, f32[2,72,128]{2,1,0:T(8,128)}, f32[3,1152]{1,0:T(4,128)}, f32[2,1,128]{2,1,0:T(1,128)}) custom-call(bf16[16,512,128]{2,1,0:T(8,128)(2,1)} %bitcast.7, bf16[3,16,512]{2,1,0:T(8,128)(2,1)} %bitcast.9, s32[1]{0:T(128)S(6)} %copy.17.h_ref, s32[1]{0:T(128)S(6)} %copy.18.w_ref, s32[1]{0:T(128)S(6)} %copy.19.bk_ref, ...), custom_call_target="tpu_custom_call" | custom-call | flops 16000000000 | bytes 5242880 | tf_op jit(solution)/shard_map/pallas_call | solution.py:703
  59.7 2.5 %shard_map.155 = (f32[72,128]{1,0:T(8,128)}, f32[72,128]{1,0:T(8,128)}, f32[3,1152]{1,0:T(4,128)}, f32[1,128]{1,0:T(1,128)}, f32[1,128]{1,0:T(1,128)}, /*index=5*/bf16[16,512,128]{2,1,0:T(8,128)(2,1)}) custom-call(bf16[16,512,128]{2,1,0:T(8,128)(2,1)} %get-tuple-element.16.gl_in, f32[2,72,128]{2,1,0:T(8,128)} %get-tuple-element.17.gw_in, ...), custom_call_target="tpu_custom_call" | custom-call | tf_op jit(solution)/shard_map/pallas_call | solution.py:725

commit v5 on v4

--- a/solution.py
+++ b/solution.py
@@ -227,9 +227,10 @@
         for k in range(many):
             stage_input(many * g + k)
 
-    loop(0, 2, stage_inputs)
+    stage_inputs(0)
     pl.semaphore_wait(barrier, ndp + nslab - 2)
     exchange_start(latent_halo)
+    stage_inputs(1)
 
     for copy in loads:
         copy.wait()

time: 62.7 us -> 61.9 us (0.987)
  Pallas kernels: 59.7 us -> 59 us
    pallas_call x1, Pallas kernels: 57.2 us -> 56.4 us  [shards(): pl.pallas_call(functools.partial(kernel, ndp, nslab, rows, width, pixel_s...]
where the time goes in v5:
time: 61.9 us; the launch traced here: 61.7 us
  Pallas kernels  59 us (95%)
  between operations  2.74 us (4%)
    pallas_call x1, Pallas kernels, shards(): pl.pallas_call(functools.partial(kernel, ndp, nslab, rows, width, pixel_s...  56.4 us
    pallas_call x1, Pallas kernels, shards(): pl.pallas_call(functools.partial(unload, parts), out_shape=(jax.ShapeDtyp...  2.53 us

profile of v5, /device:TPU:0, one launch (start us, length us, event | category | flops | bytes accessed | tf_op | source)
XLA Modules:
  0.0 61.7 jit_solution(7377668612509002349)
XLA Ops:
  2.6 56.4 %shard_map.154 = (bf16[16,512,128]{2,1,0:T(8,128)(2,1)}, f32[2,72,128]{2,1,0:T(8,128)}, f32[3,1152]{1,0:T(4,128)}, f32[2,1,128]{2,1,0:T(1,128)}) custom-call(bf16[16,512,128]{2,1,0:T(8,128)(2,1)} %bitcast.7, bf16[3,16,512]{2,1,0:T(8,128)(2,1)} %bitcast.9, s32[1]{0:T(128)S(6)} %copy.17.h_ref, s32[1]{0:T(128)S(6)} %copy.18.w_ref, s32[1]{0:T(128)S(6)} %copy.19.bk_ref, ...), custom_call_target="tpu_custom_call" | custom-call | flops 16000000000 | bytes 5242880 | tf_op jit(solution)/shard_map/pallas_call | solution.py:704
  59.0 2.5 %shard_map.155 = (f32[72,128]{1,0:T(8,128)}, f32[72,128]{1,0:T(8,128)}, f32[3,1152]{1,0:T(4,128)}, f32[1,128]{1,0:T(1,128)}, f32[1,128]{1,0:T(1,128)}, /*index=5*/bf16[16,512,128]{2,1,0:T(8,128)(2,1)}) custom-call(bf16[16,512,128]{2,1,0:T(8,128)(2,1)} %get-tuple-element.16.gl_in, f32[2,72,128]{2,1,0:T(8,128)} %get-tuple-element.17.gw_in, ...), custom_call_target="tpu_custom_call" | custom-call | tf_op jit(solution)/shard_map/pallas_call | solution.py:726

commit v6 on v5

--- a/solution.py
+++ b/solution.py
@@ -326,6 +326,13 @@
 
     loop(1, npair - 1, stage_two, 3)
 
+    def transposed(src, off, dst, lo, hi, unroll):
+        def body(row):
+            dst[row] = src[row + off, 1:t_count + 1].reshape(width, C).T
+        loop(lo, hi, body, unroll)
+
+    transposed(act, 1, actt, 1, last, 4)
+
     exchange_wait(latent_halo)
 
     @pl.when(slab == 0)
@@ -423,14 +430,10 @@
     small_c[...] = flat[0:48].astype(BF16)
     to_core(small_c, small_rc, 0).start()
 
-    def transposed(src, off, dst):
-        def body(row):
-            dst[row] = src[row + off, 1:t_count + 1].reshape(width, C).T
-        loop(0, last + 1, body, 3)
-
     slopes(latp, 0, slope0)
-    transposed(mid, 0, midt)
-    transposed(act, 1, actt)
+    transposed(mid, 0, midt, 0, last + 1, 3)
+    for row in (0, last):
+        actt[row] = act[row + 1, 1:t_count + 1].reshape(width, C).T
     wait()
 
     total = stat_total(1)

time: 61.9 us -> 61.9 us (level)
  no operation moved by 1% of the time
where the time goes in v6:
time: 61.9 us; the launch traced here: 61.6 us
  Pallas kernels  58.8 us (95%)
  between operations  2.74 us (4%)
    pallas_call x1, Pallas kernels, shards(): pl.pallas_call(functools.partial(kernel, ndp, nslab, rows, width, pixel_s...  56.3 us
    pallas_call x1, Pallas kernels, shards(): pl.pallas_call(functools.partial(unload, parts), out_shape=(jax.ShapeDtyp...  2.53 us

profile of v6, /device:TPU:0, one launch (start us, length us, event | category | flops | bytes accessed | tf_op | source)
XLA Modules:
  0.0 61.6 jit_solution(12714396588757089612)
XLA Ops:
  2.6 56.3 %shard_map.154 = (bf16[16,512,128]{2,1,0:T(8,128)(2,1)}, f32[2,72,128]{2,1,0:T(8,128)}, f32[3,1152]{1,0:T(4,128)}, f32[2,1,128]{2,1,0:T(1,128)}) custom-call(bf16[16,512,128]{2,1,0:T(8,128)(2,1)} %bitcast.7, bf16[3,16,512]{2,1,0:T(8,128)(2,1)} %bitcast.9, s32[1]{0:T(128)S(6)} %copy.17.h_ref, s32[1]{0:T(128)S(6)} %copy.18.w_ref, s32[1]{0:T(128)S(6)} %copy.19.bk_ref, ...), custom_call_target="tpu_custom_call" | custom-call | flops 16000000000 | bytes 5242880 | tf_op jit(solution)/shard_map/pallas_call | solution.py:707
  58.9 2.5 %shard_map.155 = (f32[72,128]{1,0:T(8,128)}, f32[72,128]{1,0:T(8,128)}, f32[3,1152]{1,0:T(4,128)}, f32[1,128]{1,0:T(1,128)}, f32[1,128]{1,0:T(1,128)}, /*index=5*/bf16[16,512,128]{2,1,0:T(8,128)(2,1)}) custom-call(bf16[16,512,128]{2,1,0:T(8,128)(2,1)} %get-tuple-element.16.gl_in, f32[2,72,128]{2,1,0:T(8,128)} %get-tuple-element.17.gw_in, ...), custom_call_target="tpu_custom_call" | custom-call | tf_op jit(solution)/shard_map/pallas_call | solution.py:729
